TPU v7x, 512 devices: a whole 4x8x8 slice. The times are simulated.
512 devices in a mesh: group: 64 (over y, x, core), head: 8 (over z).
Axes of the slice: x: 4, y: 8, z: 8, core: 2. Of those that a mesh axis runs over, the one named last changes fastest.
Arguments:
- queries: bfloat16 [4096, 3072], P(('group', 'head')), may hold values from -9 to 9
- key_rows: bfloat16 [4096, 3072], P(('group', 'head')), may hold values from -6 to 6
- value_rows: bfloat16 [4096, 3072], P(('group', 'head')), may hold values from -6 to 6
- latent: float32 [4096, 3072], P(('group', 'head')), may hold values from -6 to 6
- fresh_noise: float32 [4096, 3072], P(('group', 'head')), may hold values from -6 to 6
- time_index: int32 [64], replicated, may hold values from 0 to 31
- lengths: int32 [64], replicated, may hold values from 1 to 64, 2560 in all
- visible: int32 [64, 64], replicated, may hold values 0 or 1
- time_gate: float32 [32, 3072], replicated, may hold values from 0.5 to 4
- step_size: float32 [32], replicated, may hold values from 0.25 to 1
- noise_level: float32 [32], replicated, may hold values from 0.1 to 0.5
Outputs:
- latent_next: float32 [4096, 3072], P(('group', 'head'))
Inputs may be any that keep to these rules, and one draw needn't show every extreme that they name: `lengths`: some group is full.
All inputs are finite; a program needn't handle non-finite values.
Results may differ from a plain program's by a relative error of at most 0.0045.
Values may be sent and summed in bfloat16 or wider, within the bound.
No kernel may reach another device: no remote copies, remote signals or barrier semaphores. Data moves between devices by JAX's collectives and lax.ppermute only.
A program may use at most 64 MiB of HBM per device.

v0:
```python
import jax
import jax.numpy as jnp
from jax import lax
from jax.sharding import PartitionSpec as P

HD = 128


def table_lookup(table, index):
    columns = jnp.arange(table.shape[0], dtype=jnp.int32)
    return jnp.sum(jnp.where(index[:, None] == columns[None, :], table[None, :], 0), axis=1)


def local(
    queries,
    key_rows,
    value_rows,
    latent,
    fresh_noise,
    time_index,
    lengths,
    visible,
    time_gate,
    step_size,
    noise_level,
):
    head_queries, head_keys, head_values = (
        lax.all_to_all(queries, "head", split_axis=1, concat_axis=0, tiled=True),
        lax.all_to_all(key_rows, "head", split_axis=1, concat_axis=0, tiled=True),
        lax.all_to_all(value_rows, "head", split_axis=1, concat_axis=0, tiled=True),
    )
    group_len = head_queries.shape[0]
    local_heads = head_queries.shape[1] // HD
    own_group = lax.axis_index("group")
    scale = HD ** (-0.5)
    query_heads = head_queries.reshape(group_len, local_heads, HD)
    seen_row = lax.dynamic_index_in_dim(visible, own_group, 0, keepdims=False)
    key_piece = lax.all_gather(head_keys, "group", axis=0, tiled=True)
    value_piece = lax.all_gather(head_values, "group", axis=0, tiled=True)
    count = key_piece.shape[0]
    position = jnp.arange(count, dtype=jnp.int32)
    key_group = jnp.floor_divide(position, group_len)
    key_offset = position - key_group * group_len
    live = key_offset < table_lookup(lengths, key_group)
    seen = table_lookup(seen_row, key_group) == 1
    earlier = (key_group < own_group) & (key_group >= 0) & seen
    allowed = ((key_group == own_group) | earlier) & live
    scores = (
        jnp.einsum(
            "qhd,khd->hqk",
            query_heads,
            key_piece.reshape(count, local_heads, HD),
            preferred_element_type=jnp.float32,
        )
        * scale
    )
    scores = jnp.where(allowed[None, None, :], scores, -1e30)
    running = jnp.full((local_heads, group_len), -1e30, jnp.float32)
    top = jnp.maximum(running, jnp.max(scores, axis=-1))
    weights = jnp.where(allowed[None, None, :], jnp.exp(scores - top[:, :, None]), 0.0)
    total = jnp.sum(weights, axis=-1)
    update = jnp.einsum(
        "hqk,khd->qhd",
        weights.astype(jnp.bfloat16),
        value_piece.reshape(count, local_heads, HD),
        preferred_element_type=jnp.float32,
    )
    accum = update
    state = (top, total, accum)
    running, total, accum = state
    mixed = (
        (accum / jnp.transpose(total)[:, :, None])
        .reshape(group_len, local_heads * HD)
        .astype(jnp.bfloat16)
    )
    returned = lax.all_to_all(mixed, "head", split_axis=0, concat_axis=1, tiled=True)
    time_now = lax.dynamic_index_in_dim(time_index, own_group, 0, keepdims=False)
    gate_row = lax.dynamic_index_in_dim(time_gate, time_now, 0, keepdims=False)
    step_now = lax.dynamic_index_in_dim(step_size, time_now, 0, keepdims=False)
    level_now = lax.dynamic_index_in_dim(noise_level, time_now, 0, keepdims=False)
    length_now = lax.dynamic_index_in_dim(lengths, own_group, 0, keepdims=False)
    token_count = returned.shape[0]
    offsets = lax.axis_index("head") * token_count + jnp.arange(token_count, dtype=jnp.int32)
    live_rows = (offsets < length_now).astype(jnp.float32)[:, None]
    velocity = returned.astype(jnp.float32) * gate_row[None, :] * live_rows
    return latent + step_now * velocity + level_now * fresh_noise


def solution(mesh):
    placed = (
        P(("group", "head"), None),
        P(("group", "head"), None),
        P(("group", "head"), None),
        P(("group", "head"), None),
        P(("group", "head"), None),
        P(),
        P(),
        P(),
        P(),
        P(),
        P(),
    )
    return jax.shard_map(
        local, mesh=mesh, in_specs=placed, out_specs=P(("group", "head"), None), check_vma=False
    )
```

profile of v0, /device:TPU:1, one launch (start us, length us, event | category | flops | bytes accessed | tf_op | source)
XLA Modules:
  0.0 223.6 jit_solution(1631186572006772680)
XLA Ops:
  6.5 0.0 copy-start
  6.5 0.0 all-gather.3.cloned.1.call-start
  6.5 18.1 %all_to_all.64 = bf16[8,8,384]{2,0,1:T(8,128)(2,1)} all-to-all(bf16[8,8,384]{2,0,1:T(8,128)(2,1)} %bitcast.38), channel_id=1, replica_groups=mesh['group'=64,'head'=8] {'head'}, dimensions={1} | all-to-all | bytes 98304 | tf_op jit(solution)/shard_map/all_to_all | solution.py:29
  24.7 0.0 all-gather.3.cloned.1.call-update
  24.7 0.0 all-gather.5.cloned.1.call-start
  24.8 11.0 %all_to_all.65 = bf16[8,8,384]{2,0,1:T(8,128)(2,1)} all-to-all(bf16[8,8,384]{2,0,1:T(8,128)(2,1)} %bitcast.39), channel_id=1, replica_groups=mesh['group'=64,'head'=8] {'head'}, dimensions={1} | all-to-all | bytes 98304 | tf_op jit(solution)/shard_map/all_to_all | solution.py:30
  35.8 0.0 all-gather.5.cloned.1.call-update
  35.8 3.4 %all-to-all-start = ((bf16[8,8,384]{2,0,1:T(8,128)(2,1)}), bf16[8,8,384]{2,0,1:T(8,128)(2,1)S(1)}, u32[]{:S(2)}, u32[]{:S(2)}) async-start(bf16[8,8,384]{2,0,1:T(8,128)(2,1)} %bitcast.40), calls=%async_computation | async-start | bytes 98304 | tf_op jit(solution)/shard_map/all_to_all | solution.py:28
  39.2 1.2 dynamic_slice.22
  42.4 0.7 dynamic-slice_bitcast_fusion
  43.1 1.0 select_reduce_fusion.1
  44.0 0.0 copy-done
  44.1 1.3 dynamic_slice.26
  45.4 1.3 dynamic_slice.23
  46.7 1.2 dynamic_slice.27
  48.0 0.0 all-to-all-done
  48.0 0.6 reshape.80
  48.6 57.8 %all-gather.3.cloned.1.call-done = bf16[4096,384]{1,0:T(8,128)(2,1)} async-done(((bf16[64,384]{1,0:T(8,128)(2,1)}), bf16[4096,384]{1,0:T(8,128)(2,1)}) %all-gather.3.cloned.1.call-update) | async-done | bytes 3145744 | tf_op jit(solution)/shard_map/all_gather | solution.py:38
  106.4 4.9 %copy.24 = bf16[4096,384]{0,1:T(8,128)(2,1)} copy(bf16[4096,384]{1,0:T(8,128)(2,1)} %all-gather.3.cloned.1.call-done) | data formatting | bytes 6291456 | tf_op jit(solution)/shard_map/all_gather | solution.py:38
  111.3 2.9 %fusion.23 = (f32[3,64]{1,0:T(4,128)S(1)}, f32[3,64,4096]{2,1,0:T(8,128)S(1)}) fusion(bf16[4096,3,128]{0,2,1:T(8,128)(2,1)} %bitcast.31, bf16[64,3,128]{2,1,0:T(4,128)(2,1)} %reshape.80, pred[4096]{0:T(1024)(128)(4,1)S(1)} %fusion.20), kind=kOutput, calls=%fused_computation.31 | convolution fusion | flops 203685696 | bytes 6345472 | tf_op jit(solution)/shard_map/qhd,khd->hqk/dot_general | solution.py:49
  114.2 0.0 copy-start.1
  114.2 0.6 copy-done.1
  114.8 1.3 fusion.1
  116.1 75.0 %all-gather.5.cloned.1.call-done = bf16[4096,384]{1,0:T(8,128)(2,1)} async-done(((bf16[64,384]{1,0:T(8,128)(2,1)}), bf16[4096,384]{1,0:T(8,128)(2,1)}) %all-gather.5.cloned.1.call-update) | async-done | bytes 3145744 | tf_op jit(solution)/shard_map/all_gather | solution.py:39
  191.1 4.7 %copy.27 = bf16[4096,384]{0,1:T(8,128)(2,1)} copy(bf16[4096,384]{1,0:T(8,128)(2,1)} %all-gather.5.cloned.1.call-done) | data formatting | bytes 6291456 | tf_op jit(solution)/shard_map/all_gather | solution.py:39
  195.8 3.1 %fusion.14 = bf16[64,3,128]{2,0,1:T(8,128)(2,1)S(1)} fusion(bf16[4096,3,128]{0,2,1:T(8,128)(2,1)} %bitcast.32, f32[3,64,4096]{2,1,0:T(8,128)S(1)} %get-tuple-element.8, f32[3,64]{1,0:T(4,128)} %copy-done.1, pred[4096]{0:T(1024)(128)(4,1)S(1)} %fusion.20, f32[64,3]{0,1:T(4,128)} %bitcast.41), kind=kOutput, calls=%fused_computation.11 | convolution fusion | flops 203735040 | bytes 6346240 | tf_op jit(solution)/shard_map/hqk,khd->qhd/dot_general | solution.py:62
  199.0 0.7 convert_element_type.28
  199.7 7.1 %all-to-all-start.3 = ((bf16[8,8,384]{2,1,0:T(8,128)(2,1)}), bf16[8,8,384]{2,1,0:T(8,128)(2,1)S(1)}, u32[]{:S(2)}, u32[]{:S(2)}) async-start(bf16[8,8,384]{2,1,0:T(8,128)(2,1)} %convert_element_type.28), calls=%async_computation.3 | async-start | bytes 98304 | tf_op jit(solution)/shard_map/all_to_all | solution.py:76
  206.8 0.7 compare_convert_fusion
  207.5 6.4 %all-to-all-done.3 = bf16[8,8,384]{2,1,0:T(8,128)(2,1)S(1)} async-done(((bf16[8,8,384]{2,1,0:T(8,128)(2,1)}), bf16[8,8,384]{2,1,0:T(8,128)(2,1)S(1)}, u32[]{:S(2)}, u32[]{:S(2)}) %all-to-all-start.3) | async-done | bytes 49184 | tf_op jit(solution)/shard_map/all_to_all | solution.py:76
  213.8 2.9 %multiply_add_fusion = f32[8,3072]{1,0:T(8,128)} fusion(f32[8,3072]{1,0:T(8,128)} %param.15, f32[8,3072]{1,0:T(8,128)} %param.14, f32[8,3072]{1,0:T(8,128)S(1)} %bitcast.33, f32[]{:T(128)} %bitcast.19, f32[8]{0:T(128)S(1)} %compare_convert_fusion, f32[3072]{0:T(1024)S(1)} %bitcast.37, f32[]{:T(128)} %bitcast.1), kind=kLoop, calls=%fused_computation.15 | loop fusion | flops 147456 | bytes 405544 | tf_op jit(solution)/shard_map/add | solution.py:86
  (6 shorter events, 0.1 us)
Async XLA Ops:
  6.5 37.5 %copy-start = (f32[32,3072]{1,0:T(8,128)S(1)}, f32[32,3072]{1,0:T(8,128)}, u32[]{:S(2)}) copy-start(f32[32,3072]{1,0:T(8,128)} %param.19) | copy-start | bytes 1179652
  6.5 99.9 %all-gather.3.cloned.1.call-start = ((), (), s32[]{:S(2)}) async-start(), calls=%async_computation.4 | async-start | bytes 3194880 | tf_op jit(solution)/shard_map/all_gather | solution.py:38
  24.7 166.4 %all-gather.5.cloned.1.call-start = ((), (), s32[]{:S(2)}) async-start(), calls=%async_computation.5 | async-start | bytes 3194880 | tf_op jit(solution)/shard_map/all_gather | solution.py:39
  35.8 12.2 %all-to-all-start = ((bf16[8,8,384]{2,0,1:T(8,128)(2,1)}), bf16[8,8,384]{2,0,1:T(8,128)(2,1)S(1)}, u32[]{:S(2)}, u32[]{:S(2)}) async-start(bf16[8,8,384]{2,0,1:T(8,128)(2,1)} %bitcast.40), calls=%async_computation | async-start | bytes 98304 | tf_op jit(solution)/shard_map/all_to_all | solution.py:28
  114.2 0.6 copy-start.1
  199.7 14.2 %all-to-all-start.3 = ((bf16[8,8,384]{2,1,0:T(8,128)(2,1)}), bf16[8,8,384]{2,1,0:T(8,128)(2,1)S(1)}, u32[]{:S(2)}, u32[]{:S(2)}) async-start(bf16[8,8,384]{2,1,0:T(8,128)(2,1)} %convert_element_type.28), calls=%async_computation.3 | async-start | bytes 98304 | tf_op jit(solution)/shard_map/all_to_all | solution.py:76
Sparse Core Ops, SparseCore 0:
  24.8 81.5 all-gather.2
  109.8 81.2 all-gather.4
where the time goes:
time: 224 us
  waiting for transfers between devices  139 us (62%)
  blocking collectives  29.2 us (13%)
  local copies, waits for them, and re-layouts  17.4 us (8%)
  between operations  15.4 us (7%)
  starting transfers between devices  10.5 us (5%)
  matrix products  6.05 us (3%)
  other arithmetic  5.9 us (3%)
    all_gather x1, waiting for transfers between devices, local(): value_piece = lax.all_gather(head_values, 'group', axis=0, tiled=True)  75 us
    all_gather x1, waiting for transfers between devices, local(): key_piece = lax.all_gather(head_keys, 'group', axis=0, tiled=True)  57.8 us
    all_to_all x1, blocking collectives, local(): lax.all_to_all(key_rows, 'head', split_axis=1, concat_axis=0, tiled=True)  18.1 us
    all_to_all x1, blocking collectives, local(): lax.all_to_all(value_rows, 'head', split_axis=1, concat_axis=0, tiled=True)  11 us
    all_to_all x1, starting transfers between devices, local(): lax.all_to_all(mixed, 'head', split_axis=0, concat_axis=1, tiled=True)  7.1 us
    all_to_all x1, waiting for transfers between devices, local(): lax.all_to_all(mixed, 'head', split_axis=0, concat_axis=1, tiled=True)  6.36 us
    all_gather x1, local copies, waits for them, and re-layouts, local(): key_piece = lax.all_gather(head_keys, 'group', axis=0, tiled=True)  4.87 us
    all_gather x1, local copies, waits for them, and re-layouts, local(): value_piece = lax.all_gather(head_values, 'group', axis=0, tiled=True)  4.72 us
  transfers between devices with their start and end apart: 4, of which 3 were waited for; matrix products, arithmetic and copies ran while one was open for 8% of the time, Pallas kernels for 0%

commit v1 on v0

v1 whole, which is shorter than its diff:
```python
import functools

import jax
import jax.numpy as jnp
from jax import lax
from jax.experimental import pallas as pl
from jax.experimental.pallas import tpu as pltpu
from jax.sharding import Mesh
from jax.sharding import PartitionSpec as P

HD = 128
SLOTS = 64
GRID = 8
HEADS = 3
WIDE = HEADS * HD
LOW = -(2.0**100)
CHUNK = 4
LOG2E = 1.4426950408889634
LIMIT = pltpu.CompilerParams(vmem_limit_bytes=16 * 2**20)


def attend(q_ref, kv_ref, lengths_ref, visible_ref, out_ref):
    row = lax.axis_index("y")
    column = lax.axis_index("x") * 2 + lax.axis_index("core")
    keys = GRID * SLOTS
    lane = lax.broadcasted_iota(jnp.int32, (1, keys), 1)
    key_group = lane // SLOTS
    key_offset = lane - key_group * SLOTS
    alive = jnp.zeros((1, keys), jnp.int32)
    for j in range(GRID):
        alive = jnp.where(key_group == j, lengths_ref[row * GRID + j], alive)
    alive = key_offset < alive
    bias = []
    for i in range(GRID):
        own = i * GRID + column
        seen = jnp.zeros((1, keys), jnp.int32)
        for j in range(GRID):
            other = row * GRID + j
            flag = jnp.where(other < own, visible_ref[own, other], 0)
            flag = jnp.where(other == own, 1, flag)
            seen = jnp.where(key_group == j, flag, seen)
        bias.append(jnp.where((seen == 1) & alive, 0.0, LOW))
    spot = lax.broadcasted_iota(jnp.int32, (SLOTS, HD), 1)
    stats = [jnp.zeros((SLOTS, HD), jnp.float32)] * GRID
    ones = jnp.ones((keys, HD), jnp.bfloat16)
    for h in range(HEADS):
        part = slice(h * HD, (h + 1) * HD)
        values = jnp.concatenate([kv_ref[:, WIDE + h * HD : WIDE + (h + 1) * HD], ones], axis=1)
        for c in range(0, GRID, CHUNK):
            scores = lax.dot_general(
                q_ref[c : c + CHUNK, :, part].reshape(CHUNK * SLOTS, HD),
                kv_ref[:, part],
                (((1,), (1,)), ((), ())),
                preferred_element_type=jnp.float32,
            )
            raw, tops = [], []
            for i in range(CHUNK):
                score = scores[i * SLOTS : (i + 1) * SLOTS] * (HD**-0.5 * LOG2E) + bias[c + i]
                top = jnp.max(score, axis=1, keepdims=True)
                top = top.astype(jnp.bfloat16).astype(jnp.float32)
                raw.append(jnp.exp2(score - top).astype(jnp.bfloat16))
                tops.append(top)
            mixed = jnp.dot(
                jnp.concatenate(raw, axis=0), values, preferred_element_type=jnp.float32
            )
            for i in range(CHUNK):
                block = mixed[i * SLOTS : (i + 1) * SLOTS]
                out_ref[c + i, :, part] = block[:, :HD].astype(jnp.bfloat16)
                total = block[:, HD:]
                coarse = total.astype(jnp.bfloat16).astype(jnp.float32)
                stat = stats[c + i]
                stat = jnp.where(spot == h, tops[i], stat)
                stat = jnp.where(spot == h + 32, coarse, stat)
                stats[c + i] = jnp.where(spot == h + 64, total - coarse, stat)
    for i in range(GRID):
        out_ref[i, :, WIDE:] = stats[i].astype(jnp.bfloat16)


def update(time_ref, length_ref, step_ref, level_ref, part_ref, latent_ref, noise_ref, gate_ref, out_ref):
    group = (lax.axis_index("y") * 4 + lax.axis_index("x")) * 2 + lax.axis_index("core")
    now = time_ref[group]
    step = step_ref[now]
    level = level_ref[now]
    rows = latent_ref.shape[0]
    offset = lax.axis_index("head") * rows + lax.broadcasted_iota(jnp.int32, (rows, HD), 0)
    live = offset < length_ref[group]
    gate_rows = gate_ref[...]
    pick = lax.broadcasted_iota(jnp.int32, gate_rows.shape, 0) == now
    gate = jnp.sum(jnp.where(pick, gate_rows, 0.0), axis=0, keepdims=True)
    for g in range(GRID):
        stats = [part_ref[b * GRID + g, :, WIDE:].astype(jnp.float32) for b in range(GRID)]
        top = functools.reduce(jnp.maximum, stats)
        scale = [jnp.exp2(s - top) for s in stats]
        sums = [pltpu.roll(s, HD - 32, 1) + pltpu.roll(s, HD - 64, 1) for s in stats]
        total = functools.reduce(jnp.add, [w * s for w, s in zip(scale, sums)])
        for h in range(HEADS):
            part = slice(h * HD, (h + 1) * HD)
            mixed = functools.reduce(
                jnp.add,
                [
                    scale[b][:, h : h + 1] * part_ref[b * GRID + g, :, part].astype(jnp.float32)
                    for b in range(GRID)
                ],
            )
            mixed = mixed / total[:, h : h + 1]
            place = slice((g * HEADS + h) * HD, (g * HEADS + h + 1) * HD)
            velocity = jnp.where(live, mixed * gate[:, place], 0.0)
            out_ref[:, place] = (
                latent_ref[:, place] + step * velocity + level * noise_ref[:, place]
            )


def local(
    queries,
    key_rows,
    value_rows,
    latent,
    fresh_noise,
    time_index,
    lengths,
    visible,
    time_gate,
    step_size,
    noise_level,
):
    rows = queries.shape[0]
    vmem = pl.BlockSpec(memory_space=pltpu.VMEM)
    smem = pl.BlockSpec(memory_space=pltpu.SMEM)
    mine = jnp.concatenate(
        [a.reshape(rows, GRID, WIDE).swapaxes(0, 1) for a in (key_rows, value_rows, queries)],
        axis=2,
    )
    mine = lax.all_to_all(mine, "head", split_axis=0, concat_axis=0, tiled=True)
    mine = mine.reshape(SLOTS, 3 * WIDE)
    keys_values = lax.all_gather(mine[:, : 2 * WIDE], ("x", "core"), axis=0, tiled=True)
    head_queries = lax.all_to_all(
        jnp.broadcast_to(mine[None, :, 2 * WIDE :], (GRID, SLOTS, WIDE)),
        "y",
        split_axis=0,
        concat_axis=0,
        tiled=True,
    )
    partial = pl.pallas_call(
        attend,
        out_shape=jax.ShapeDtypeStruct((GRID, SLOTS, WIDE + HD), jnp.bfloat16),
        in_specs=[vmem, vmem, smem, smem],
        out_specs=vmem,
        compiler_params=LIMIT,
    )(head_queries, keys_values, lengths, visible)
    partial = lax.all_to_all(
        partial.reshape(GRID * GRID, rows, WIDE + HD),
        ("y", "head"),
        split_axis=0,
        concat_axis=0,
        tiled=True,
    )
    return pl.pallas_call(
        update,
        out_shape=jax.ShapeDtypeStruct(latent.shape, jnp.float32),
        in_specs=[smem] * 4 + [vmem] * 4,
        out_specs=vmem,
        compiler_params=LIMIT,
    )(time_index, lengths, step_size, noise_level, partial, latent, fresh_noise, time_gate)


def solution(mesh):
    grid = Mesh(mesh.devices.reshape(8, 4, 2, 8), ("y", "x", "core", "head"))
    tokens = P(("y", "x", "core", "head"), None)
    placed = (tokens,) * 5 + (P(),) * 6
    return jax.shard_map(local, mesh=grid, in_specs=placed, out_specs=tokens, check_vma=False)
```

time: 224 us -> 75.1 us (0.34)
  the two profiles are of different devices: /device:TPU:1 before, /device:TPU:16 now
where the time goes in v1:
time: 75.1 us; the launch traced here: 74.8 us
  blocking collectives  61 us (81%)
  starting transfers between devices  7.43 us (10%)
  Pallas kernels  4.54 us (6%)
  other arithmetic  0.86 us (1%)
  local copies, waits for them, and re-layouts  0.83 us (1%)
    all_to_all x1, blocking collectives, local(): lax.all_to_all(partial.reshape(GRID * GRID, rows, WIDE + HD), ('y', 'head...  27.6 us
    all_to_all x1, blocking collectives, local(): mine = lax.all_to_all(mine, 'head', split_axis=0, concat_axis=0, tiled=True)  19.5 us
    all_gather x1, blocking collectives, local(): lax.all_gather(mine[:, :2 * WIDE], ('x', 'core'), axis=0, tiled=True)  13.8 us
    all_to_all x1, starting transfers between devices, local(): lax.all_to_all(jnp.broadcast_to(mine[None, :, 2 * WIDE:], (GRID, SLOTS, W...  7.43 us
    pallas_call x1, Pallas kernels, local(): pl.pallas_call(attend, out_shape=jax.ShapeDtypeStruct((GRID, SLOTS, WIDE...  2.41 us
    pallas_call x1, Pallas kernels, local(): pl.pallas_call(update, out_shape=jax.ShapeDtypeStruct(latent.shape, jnp.f...  2.14 us
  transfers between devices with their start and end apart: 1, of which 0 were waited for; matrix products, arithmetic and copies ran while one was open for 0% of the time, Pallas kernels for 0%

profile of v1, /device:TPU:16, one launch (start us, length us, event | category | flops | bytes accessed | tf_op | source)
XLA Modules:
  0.0 74.8 jit_solution(5014114166335206325)
XLA Ops:
  0.0 0.9 %pad_maximum_fusion = bf16[8,8,1152]{2,1,0:T(8,128)(2,1)S(1)} fusion(bf16[8,8,384]{2,1,0:T(8,128)(2,1)} %bitcast.14, bf16[8,8,384]{2,1,0:T(8,128)(2,1)} %bitcast.15, bf16[8,8,384]{2,1,0:T(8,128)(2,1)} %bitcast.16), kind=kLoop, calls=%fused_computation | loop fusion | flops 442368 | bytes 294912 | tf_op jit(solution)/shard_map/concatenate | solution.py:129
  0.9 19.5 %all_to_all.15 = bf16[8,8,1152]{2,1,0:T(8,128)(2,1)S(1)} all-to-all(bf16[8,8,1152]{2,1,0:T(8,128)(2,1)S(1)} %pad_maximum_fusion), channel_id=1, replica_groups=mesh['y'=8,'x'=4,'core'=2,'head'=8] {'head'}, dimensions={0} | all-to-all | bytes 294912 | tf_op jit(solution)/shard_map/all_to_all | solution.py:133
  20.4 0.8 %broadcast_in_dim.2 = bf16[8,64,384]{2,1,0:T(8,128)(2,1)} broadcast(bf16[64,384]{1,0:T(8,128)(2,1)S(1)} %slice.8), dimensions={1,2} | broadcast | bytes 442368 | tf_op jit(solution)/shard_map/broadcast_in_dim | solution.py:137
  21.2 7.4 %all-to-all-start.1 = ((bf16[8,64,384]{2,1,0:T(8,128)(2,1)}), bf16[8,64,384]{2,1,0:T(8,128)(2,1)S(1)}, u32[]{:S(2)}, u32[]{:S(2)}) async-start(bf16[8,64,384]{2,1,0:T(8,128)(2,1)} %broadcast_in_dim.2), calls=%async_computation.1 | async-start | bytes 786432 | tf_op jit(solution)/shard_map/all_to_all | solution.py:136
  28.6 0.0 copy-start.3
  28.6 0.0 copy-start.4
  28.6 13.8 %all_gather.3.kv_ref = bf16[512,768]{1,0:T(8,128)(2,1)S(1)} all-gather(bf16[64,768]{1,0:T(8,128)(2,1)S(1)} %slice.9), channel_id=1, replica_groups=mesh['y'=8,'x'=4,'core'=2,'head'=8] {'x','core'}, dimensions={0}, use_global_device_ids=true | all-gather | bytes 884736 | tf_op jit(solution)/shard_map/all_gather | solution.py:135
  42.5 0.0 all-to-all-done.1.q_ref
  42.5 0.0 copy-done.3
  42.5 0.0 copy-done.4
  42.5 2.4 %shard_map.109 = bf16[8,64,512]{2,1,0:T(8,128)(2,1)S(1)} custom-call(bf16[8,64,384]{2,1,0:T(8,128)(2,1)S(1)} %all-to-all-done.1.q_ref, bf16[512,768]{1,0:T(8,128)(2,1)S(1)} %all_gather.3.kv_ref, s32[64]{0:T(128)S(1)} %copy-done.4, s32[64,64]{1,0:T(8,128)S(1)} %copy-done.3), custom_call_target="tpu_custom_call" | custom-call | tf_op jit(solution)/shard_map/pallas_call | solution.py:143
  44.9 0.0 copy-start
  44.9 0.0 copy-start.1
  44.9 0.0 copy-start.2
  44.9 0.0 copy-start.5
  44.9 0.0 copy-start.6
  45.0 0.0 copy-start.7
  45.0 27.6 %all_to_all.16.part_ref = bf16[64,8,512]{2,1,0:T(8,128)(2,1)S(1)} all-to-all(bf16[64,8,512]{2,1,0:T(8,128)(2,1)S(1)} %bitcast.11), channel_id=1, replica_groups=mesh['y'=8,'x'=4,'core'=2,'head'=8] {'y','head'}, dimensions={0} | all-to-all | bytes 1048576 | tf_op jit(solution)/shard_map/all_to_all | solution.py:150
  72.6 0.0 copy-done
  72.6 0.0 copy-done.1
  72.6 0.0 copy-done.2
  72.6 0.0 copy-done.5
  72.6 0.0 copy-done.6
  72.6 0.0 copy-done.7
  72.6 2.1 %shard_map.110 = f32[8,3072]{1,0:T(8,128)} custom-call(s32[64]{0:T(128)S(1)} %copy-done.5, s32[64]{0:T(128)S(1)} %copy-done.4, f32[32]{0:T(128)S(1)} %copy-done.6, f32[32]{0:T(128)S(1)} %copy-done.7, bf16[64,8,512]{2,1,0:T(8,128)(2,1)S(1)} %all_to_all.16.part_ref, f32[8,3072]{1,0:T(8,128)S(1)} %copy-done.1, f32[8,3072]{1,0:T(8,128)S(1)} %copy-done.2, ...), custom_call_target="tpu_custom_call" | custom-call | tf_op jit(solution)/shard_map/pallas_call | solution.py:157
  (2 shorter events, 0.0 us)
Async XLA Ops:
  21.2 21.3 %all-to-all-start.1 = ((bf16[8,64,384]{2,1,0:T(8,128)(2,1)}), bf16[8,64,384]{2,1,0:T(8,128)(2,1)S(1)}, u32[]{:S(2)}, u32[]{:S(2)}) async-start(bf16[8,64,384]{2,1,0:T(8,128)(2,1)} %broadcast_in_dim.2), calls=%async_computation.1 | async-start | bytes 786432 | tf_op jit(solution)/shard_map/all_to_all | solution.py:136
  28.6 13.9 %copy-start.3 = (s32[64,64]{1,0:T(8,128)S(1)}, s32[64,64]{1,0:T(8,128)}, u32[]{:S(2)}) copy-start(s32[64,64]{1,0:T(8,128)} %visible_ref.1) | copy-start | bytes 49156
  28.6 13.8 %copy-start.4 = (s32[64]{0:T(128)S(1)}, s32[64]{0:T(128)}, u32[]{:S(2)}) copy-start(s32[64]{0:T(128)} %length_ref.1) | copy-start | bytes 772
  44.9 27.7 %copy-start = (f32[32,3072]{1,0:T(8,128)S(1)}, f32[32,3072]{1,0:T(8,128)}, u32[]{:S(2)}) copy-start(f32[32,3072]{1,0:T(8,128)} %gate_ref.1) | copy-start | bytes 1179652
  44.9 27.7 %copy-start.1 = (f32[8,3072]{1,0:T(8,128)S(1)}, f32[8,3072]{1,0:T(8,128)}, u32[]{:S(2)}) copy-start(f32[8,3072]{1,0:T(8,128)} %latent_ref.1) | copy-start | bytes 294916
  44.9 27.7 %copy-start.2 = (f32[8,3072]{1,0:T(8,128)S(1)}, f32[8,3072]{1,0:T(8,128)}, u32[]{:S(2)}) copy-start(f32[8,3072]{1,0:T(8,128)} %noise_ref.1) | copy-start | bytes 294916
  44.9 27.7 %copy-start.5 = (s32[64]{0:T(128)S(1)}, s32[64]{0:T(128)}, u32[]{:S(2)}) copy-start(s32[64]{0:T(128)} %time_ref.1) | copy-start | bytes 772
  44.9 27.7 %copy-start.6 = (f32[32]{0:T(128)S(1)}, f32[32]{0:T(128)}, u32[]{:S(2)}) copy-start(f32[32]{0:T(128)} %step_ref.1) | copy-start | bytes 388
  45.0 27.7 %copy-start.7 = (f32[32]{0:T(128)S(1)}, f32[32]{0:T(128)}, u32[]{:S(2)}) copy-start(f32[32]{0:T(128)} %level_ref.1) | copy-start | bytes 388

commit v2 on v1

v2 whole, which is shorter than its diff:
```python
import functools

import jax
import jax.numpy as jnp
from jax import lax
from jax.experimental import pallas as pl
from jax.experimental.pallas import tpu as pltpu
from jax.sharding import Mesh
from jax.sharding import PartitionSpec as P

HD = 128
HEADS = 3
WIDE = HEADS * HD
SETS = 8
BANDS = 4
ROWS = 8
LOW = -(2.0**100)
LOG2E = 1.4426950408889634
LIMIT = pltpu.CompilerParams(vmem_limit_bytes=16 * 2**20)


def prepare(
    time_ref, length_ref, step_ref, level_ref, visible_ref, latent_ref, noise_ref, gate_ref,
    mine_ref, theirs_ref, base_ref, slope_ref,
):
    band = lax.axis_index("yh")
    core = lax.axis_index("core")
    blocks = BANDS * SETS
    keys = mine_ref.shape[1]
    groups = visible_ref.shape[0]
    lane = lax.broadcasted_iota(jnp.int32, (1, keys), 1)
    key_set = (lane // ROWS) % SETS
    key_offset = lane // (ROWS * SETS) * ROWS + lane % ROWS
    own = lax.broadcasted_iota(jnp.int32, (blocks, 1), 0) * 2 + core
    pick = own == lax.broadcasted_iota(jnp.int32, (blocks, groups), 1)
    rows = jnp.dot(
        pick.astype(jnp.bfloat16),
        visible_ref[...].astype(jnp.float32).astype(jnp.bfloat16),
        preferred_element_type=jnp.float32,
    ).astype(jnp.bfloat16)
    for key_core, bias_ref in ((core, mine_ref), (1 - core, theirs_ref)):
        key_group = band * (2 * SETS) + key_set * 2 + key_core
        length = jnp.zeros((1, keys), jnp.int32)
        for j in range(SETS):
            length = jnp.where(
                key_set == j, length_ref[band * (2 * SETS) + 2 * j + key_core], length
            )
        spread = lax.broadcasted_iota(jnp.int32, (groups, keys), 0) == key_group
        seen = jnp.dot(rows, spread.astype(jnp.bfloat16), preferred_element_type=jnp.float32)
        reach = (key_group == own) | ((key_group < own) & (seen > 0.5))
        bias = jnp.where(reach & (key_offset < length), 0.0, LOW)
        for j in range(blocks):
            bias_ref[j * ROWS : (j + 1) * ROWS, :] = jnp.broadcast_to(bias[j : j + 1], (ROWS, keys))
    group = band * 2 + lax.axis_index("yl")
    group = (group * 4 + lax.axis_index("x")) * 2 + core
    now = time_ref[group]
    offset = lax.axis_index("head") * ROWS + lax.broadcasted_iota(jnp.int32, latent_ref.shape, 0)
    pick = lax.broadcasted_iota(jnp.int32, gate_ref.shape, 0) == now
    gate = jnp.sum(jnp.where(pick, gate_ref[...], 0.0), axis=0, keepdims=True)
    slope_ref[...] = jnp.where(offset < length_ref[group], step_ref[now] * gate, 0.0)
    base_ref[...] = latent_ref[...] + level_ref[now] * noise_ref[...]


def attend(q_ref, first_ref, second_ref, *refs):
    *bias_refs, out_ref = refs
    key_refs = (first_ref, second_ref)
    queries, keys = q_ref.shape[0], first_ref.shape[0]
    spot = lax.broadcasted_iota(jnp.int32, (queries, HD), 1)
    stat = jnp.zeros((queries, HD), jnp.float32)
    ones = jnp.ones((keys, HD), jnp.bfloat16)
    for h in range(HEADS):
        part = slice(h * HD, (h + 1) * HD)
        scores = []
        for key_ref, bias_ref in zip(key_refs, bias_refs):
            score = lax.dot_general(
                q_ref[:, part],
                key_ref[:, part],
                (((1,), (1,)), ((), ())),
                preferred_element_type=jnp.float32,
            )
            scores.append(score * (HD**-0.5 * LOG2E) + bias_ref[...])
        top = jnp.max(functools.reduce(jnp.maximum, scores), axis=1, keepdims=True)
        top = top.astype(jnp.bfloat16).astype(jnp.float32)
        mixed = jnp.zeros((queries, 2 * HD), jnp.float32)
        for score, key_ref in zip(scores, key_refs):
            values = key_ref[:, WIDE + h * HD : WIDE + (h + 1) * HD]
            mixed += jnp.dot(
                jnp.exp2(score - top).astype(jnp.bfloat16),
                jnp.concatenate([values, ones], axis=1),
                preferred_element_type=jnp.float32,
            )
        out_ref[:, part] = mixed[:, :HD].astype(jnp.bfloat16)
        total = mixed[:, HD:]
        coarse = total.astype(jnp.bfloat16).astype(jnp.float32)
        stat = jnp.where(spot == h, top, stat)
        stat = jnp.where(spot == h + 32, coarse, stat)
        stat = jnp.where(spot == h + 64, total - coarse, stat)
    out_ref[:, WIDE:] = stat.astype(jnp.bfloat16)


def update(part_ref, base_ref, slope_ref, out_ref):
    for g in range(SETS):
        stats = [part_ref[b * SETS + g, :, WIDE:].astype(jnp.float32) for b in range(BANDS)]
        top = functools.reduce(jnp.maximum, stats)
        scale = [jnp.exp2(s - top) for s in stats]
        sums = [pltpu.roll(s, HD - 32, 1) + pltpu.roll(s, HD - 64, 1) for s in stats]
        total = functools.reduce(jnp.add, [w * s for w, s in zip(scale, sums)])
        scale = [w / total for w in scale]
        for h in range(HEADS):
            part = slice(h * HD, (h + 1) * HD)
            mixed = functools.reduce(
                jnp.add,
                [
                    scale[b][:, h : h + 1] * part_ref[b * SETS + g, :, part].astype(jnp.float32)
                    for b in range(BANDS)
                ],
            )
            place = slice((g * HEADS + h) * HD, (g * HEADS + h + 1) * HD)
            out_ref[:, place] = base_ref[:, place] + slope_ref[:, place] * mixed


def local(
    queries,
    key_rows,
    value_rows,
    latent,
    fresh_noise,
    time_index,
    lengths,
    visible,
    time_gate,
    step_size,
    noise_level,
):
    vmem = pl.BlockSpec(memory_space=pltpu.VMEM)
    smem = pl.BlockSpec(memory_space=pltpu.SMEM)
    mine = jnp.concatenate(
        [a.reshape(ROWS, SETS, WIDE).swapaxes(0, 1) for a in (key_rows, value_rows, queries)],
        axis=2,
    )
    mine = lax.all_to_all(mine, ("yl", "x"), split_axis=0, concat_axis=0, tiled=True)
    mine = mine.reshape(SETS * ROWS, 3 * WIDE)
    slices = lax.all_to_all(
        jnp.broadcast_to(mine[None, :, : 2 * WIDE], (SETS, SETS * ROWS, 2 * WIDE)),
        "head",
        split_axis=0,
        concat_axis=0,
        tiled=True,
    )
    head_queries = lax.all_gather(mine[:, 2 * WIDE :], "yh", axis=0, tiled=True)
    slices, head_queries = lax.optimization_barrier((slices, head_queries))
    slices = slices.reshape(-1, 2 * WIDE)
    halves = [slices, lax.ppermute(slices, "core", [(0, 1), (1, 0)])]
    rows, keys = BANDS * SETS * ROWS, SETS * SETS * ROWS
    bias = jax.ShapeDtypeStruct((rows, keys), jnp.float32)
    *biases, base, slope = pl.pallas_call(
        prepare,
        out_shape=[bias, bias] + [jax.ShapeDtypeStruct(latent.shape, jnp.float32)] * 2,
        in_specs=[smem] * 4 + [vmem] * 4,
        out_specs=[vmem] * 4,
        compiler_params=LIMIT,
        cost_estimate=pl.CostEstimate(flops=10**8, bytes_accessed=2**21, transcendentals=0),
    )(time_index, lengths, step_size, noise_level, visible, latent, fresh_noise, time_gate)
    partial = pl.pallas_call(
        attend,
        out_shape=jax.ShapeDtypeStruct((rows, WIDE + HD), jnp.bfloat16),
        in_specs=[vmem] * 5,
        out_specs=vmem,
        compiler_params=LIMIT,
    )(head_queries, *halves, *biases)
    partial = lax.all_to_all(
        partial.reshape(BANDS * SETS, ROWS, WIDE + HD),
        ("yh", "yl", "x"),
        split_axis=0,
        concat_axis=0,
        tiled=True,
    )
    return pl.pallas_call(
        update,
        out_shape=jax.ShapeDtypeStruct(latent.shape, jnp.float32),
        in_specs=[vmem] * 3,
        out_specs=vmem,
        compiler_params=LIMIT,
    )(partial, base, slope)


def solution(mesh):
    names = ("yh", "yl", "x", "core", "head")
    grid = Mesh(mesh.devices.reshape(BANDS, 2, 4, 2, 8), names)
    tokens = P(names, None)
    placed = (tokens,) * 5 + (P(),) * 6
    return jax.shard_map(local, mesh=grid, in_specs=placed, out_specs=tokens, check_vma=False)
```

time: 75.1 us -> 72.6 us (0.967)
  the two profiles are of different devices: /device:TPU:16 before, /device:TPU:8 now
where the time goes in v2:
time: 72.6 us; the launch traced here: 72.2 us
  blocking collectives  49.8 us (69%)
  starting transfers between devices  9.7 us (13%)
  waiting for transfers between devices  7.22 us (10%)
  Pallas kernels  3.56 us (5%)
  local copies, waits for them, and re-layouts  1 us (1%)
  other arithmetic  0.86 us (1%)
    all_to_all x1, blocking collectives, local(): lax.all_to_all(partial.reshape(BANDS * SETS, ROWS, WIDE + HD), ('yh', 'yl...  20.5 us
    all_gather x1, blocking collectives, local(): head_queries = lax.all_gather(mine[:, 2 * WIDE:], 'yh', axis=0, tiled=True)  15.7 us
    all_to_all x1, blocking collectives, local(): lax.all_to_all(mine, ('yl', 'x'), split_axis=0, concat_axis=0, tiled=True)  13.5 us
    all_to_all x1, starting transfers between devices, local(): lax.all_to_all(jnp.broadcast_to(mine[None, :, :2 * WIDE], (SETS, SETS * R...  7.79 us
    all_to_all x1, waiting for transfers between devices, local(): lax.all_to_all(jnp.broadcast_to(mine[None, :, :2 * WIDE], (SETS, SETS * R...  5.96 us
    ppermute x1, starting transfers between devices, local(): halves = [slices, lax.ppermute(slices, 'core', [(0, 1), (1, 0)])]  1.91 us
    pallas_call x1, Pallas kernels, local(): pl.pallas_call(attend, out_shape=jax.ShapeDtypeStruct((rows, WIDE + HD),...  1.49 us
  transfers between devices with their start and end apart: 2, of which 2 were waited for; matrix products, arithmetic and copies ran while one was open for 0% of the time, Pallas kernels for 1%

profile of v2, /device:TPU:8, one launch (start us, length us, event | category | flops | bytes accessed | tf_op | source)
XLA Modules:
  0.0 72.2 jit_solution(15250926717920578957)
XLA Ops:
  0.0 0.9 %pad_maximum_fusion = bf16[8,8,1152]{2,1,0:T(8,128)(2,1)S(1)} fusion(bf16[8,8,384]{2,1,0:T(8,128)(2,1)} %bitcast.17, bf16[8,8,384]{2,1,0:T(8,128)(2,1)} %bitcast.18, bf16[8,8,384]{2,1,0:T(8,128)(2,1)} %bitcast.19), kind=kLoop, calls=%fused_computation | loop fusion | flops 442368 | bytes 294912 | tf_op jit(solution)/shard_map/concatenate | solution.py:137
  0.9 13.5 %all_to_all.15 = bf16[8,8,1152]{2,1,0:T(8,128)(2,1)S(1)} all-to-all(bf16[8,8,1152]{2,1,0:T(8,128)(2,1)S(1)} %pad_maximum_fusion), channel_id=1, replica_groups=mesh['yh'=4,'yl'=2,'x'=4,'core'=2,'head'=8] {'yl','x'}, dimensions={0} | all-to-all | bytes 294912 | tf_op jit(solution)/shard_map/all_to_all | solution.py:141
  14.4 0.9 %broadcast_in_dim.2 = bf16[8,64,768]{2,1,0:T(8,128)(2,1)} broadcast(bf16[64,768]{1,0:T(8,128)(2,1)S(1)} %slice.8), dimensions={1,2} | broadcast | bytes 884736 | tf_op jit(solution)/shard_map/broadcast_in_dim | solution.py:144
  15.3 0.0 copy-start
  15.3 7.8 %all-to-all-start.1 = ((bf16[8,64,768]{2,1,0:T(8,128)(2,1)}), bf16[8,64,768]{2,1,0:T(8,128)(2,1)S(1)}, u32[]{:S(2)}, u32[]{:S(2)}) async-start(bf16[8,64,768]{2,1,0:T(8,128)(2,1)} %broadcast_in_dim.2), calls=%async_computation.1 | async-start | bytes 1572864 | tf_op jit(solution)/shard_map/all_to_all | solution.py:143
  23.1 0.0 copy-start.1
  23.2 0.0 copy-start.2
  23.2 0.0 copy-start.3
  23.2 0.0 copy-start.7
  23.2 15.7 %all_gather.3.q_ref = bf16[256,384]{1,0:T(8,128)(2,1)S(1)} all-gather(bf16[64,384]{1,0:T(8,128)(2,1)S(1)} %slice.9), channel_id=1, replica_groups=mesh['yh'=4,'yl'=2,'x'=4,'core'=2,'head'=8] {'yh'}, dimensions={0}, use_global_device_ids=true | all-gather | bytes 245760 | tf_op jit(solution)/shard_map/all_gather | solution.py:150
  38.9 0.0 copy-start.4
  38.9 0.0 copy-start.5
  38.9 0.0 copy-start.6
  38.9 6.0 %all-to-all-done.1 = bf16[8,64,768]{2,1,0:T(8,128)(2,1)S(1)} async-done(((bf16[8,64,768]{2,1,0:T(8,128)(2,1)}), bf16[8,64,768]{2,1,0:T(8,128)(2,1)S(1)}, u32[]{:S(2)}, u32[]{:S(2)}) %all-to-all-start.1) | async-done | bytes 786464 | tf_op jit(solution)/shard_map/all_to_all | solution.py:143
  44.8 1.9 %collective-permute-start = (bf16[512,768]{1,0:T(8,128)(2,1)S(1)}, bf16[512,768]{1,0:T(8,128)(2,1)S(1)}, u32[]{:S(2)}, u32[]{:S(2)}) collective-permute-start(bf16[512,768]{1,0:T(8,128)(2,1)S(1)} %bitcast.12), channel_id=1, source_target_pairs={{0,8},{8,0},{1,9},{9,1},{2,10},{10,2},{3,11},{11,3},{4,12},{12,4},... | collective-permute-start | bytes 2359304 | tf_op jit(solution)/shard_map/ppermute | solution.py:153
  46.8 0.0 copy-done
  46.8 0.0 copy-done.1
  46.8 0.0 copy-done.2
  46.8 0.0 copy-done.3
  46.8 0.0 copy-done.7
  46.8 0.0 copy-done.4
  46.8 0.0 copy-done.5
  46.8 0.0 copy-done.6
  46.8 0.9 %shard_map.109 = (f32[256,512]{1,0:T(8,128)S(1)}, f32[256,512]{1,0:T(8,128)S(1)}, f32[8,3072]{1,0:T(8,128)S(1)}, f32[8,3072]{1,0:T(8,128)S(1)}) custom-call(s32[64]{0:T(128)S(1)} %copy-done.4, s32[64]{0:T(128)S(1)} %copy-done.5, f32[32]{0:T(128)S(1)} %copy-done.6, f32[32]{0:T(128)S(1)} %copy-done.7, s32[64,64]{1,0:T(8,128)S(1)} %copy-done.3, ...), custom_call_target="tpu_custom_call" | custom-call | flops 100000000 | bytes 2097152 | tf_op jit(solution)/shard_map/pallas_call | solution.py:156
  47.8 1.3 %collective-permute-done.second_ref = bf16[512,768]{1,0:T(8,128)(2,1)S(1)} collective-permute-done((bf16[512,768]{1,0:T(8,128)(2,1)S(1)}, bf16[512,768]{1,0:T(8,128)(2,1)S(1)}, u32[]{:S(2)}, u32[]{:S(2)}) %collective-permute-start) | collective-permute-done | bytes 786464 | tf_op jit(solution)/shard_map/ppermute | solution.py:153
  49.0 1.5 %shard_map.110 = bf16[256,512]{1,0:T(8,128)(2,1)S(1)} custom-call(bf16[256,384]{1,0:T(8,128)(2,1)S(1)} %all_gather.3.q_ref, bf16[512,768]{1,0:T(8,128)(2,1)S(1)} %bitcast.13, bf16[512,768]{1,0:T(8,128)(2,1)S(1)} %collective-permute-done.second_ref, f32[256,512]{1,0:T(8,128)S(1)} %get-tuple-element.13.refs_0_, f32[256,512]{1,0:T(8,128)S(1)} %get-tuple-element.14.refs_1_), custom_call_target="tpu_custom_call" | custom-call | tf_op jit(solution)/shard_map/pallas_call | solution.py:164
  50.5 20.5 %all_to_all.16.part_ref = bf16[32,8,512]{2,1,0:T(8,128)(2,1)S(1)} all-to-all(bf16[32,8,512]{2,1,0:T(8,128)(2,1)S(1)} %bitcast.14), channel_id=1, replica_groups=mesh['yh'=4,'yl'=2,'x'=4,'core'=2,'head'=8] {'yh','yl','x'}, dimensions={0} | all-to-all | bytes 524288 | tf_op jit(solution)/shard_map/all_to_all | solution.py:171
  71.1 1.2 %shard_map.111 = f32[8,3072]{1,0:T(8,128)} custom-call(bf16[32,8,512]{2,1,0:T(8,128)(2,1)S(1)} %all_to_all.16.part_ref, f32[8,3072]{1,0:T(8,128)S(1)} %get-tuple-element.15.base_ref, f32[8,3072]{1,0:T(8,128)S(1)} %get-tuple-element.16.slope_ref), custom_call_target="tpu_custom_call" | custom-call | tf_op jit(solution)/shard_map/pallas_call | solution.py:178
  (2 shorter events, 0.0 us)
Async XLA Ops:
  15.3 31.4 %copy-start = (f32[32,3072]{1,0:T(8,128)S(1)}, f32[32,3072]{1,0:T(8,128)}, u32[]{:S(2)}) copy-start(f32[32,3072]{1,0:T(8,128)} %gate_ref.1) | copy-start | bytes 1179652
  15.3 29.5 %all-to-all-start.1 = ((bf16[8,64,768]{2,1,0:T(8,128)(2,1)}), bf16[8,64,768]{2,1,0:T(8,128)(2,1)S(1)}, u32[]{:S(2)}, u32[]{:S(2)}) async-start(bf16[8,64,768]{2,1,0:T(8,128)(2,1)} %broadcast_in_dim.2), calls=%async_computation.1 | async-start | bytes 1572864 | tf_op jit(solution)/shard_map/all_to_all | solution.py:143
  23.1 23.6 %copy-start.1 = (f32[8,3072]{1,0:T(8,128)S(1)}, f32[8,3072]{1,0:T(8,128)}, u32[]{:S(2)}) copy-start(f32[8,3072]{1,0:T(8,128)} %latent_ref.1) | copy-start | bytes 294916
  23.2 23.6 %copy-start.2 = (f32[8,3072]{1,0:T(8,128)S(1)}, f32[8,3072]{1,0:T(8,128)}, u32[]{:S(2)}) copy-start(f32[8,3072]{1,0:T(8,128)} %noise_ref.1) | copy-start | bytes 294916
  23.2 23.6 %copy-start.3 = (s32[64,64]{1,0:T(8,128)S(1)}, s32[64,64]{1,0:T(8,128)}, u32[]{:S(2)}) copy-start(s32[64,64]{1,0:T(8,128)} %visible_ref.1) | copy-start | bytes 49156
  23.2 23.6 %copy-start.7 = (f32[32]{0:T(128)S(1)}, f32[32]{0:T(128)}, u32[]{:S(2)}) copy-start(f32[32]{0:T(128)} %level_ref.1) | copy-start | bytes 388
  38.9 7.9 %copy-start.4 = (s32[64]{0:T(128)S(1)}, s32[64]{0:T(128)}, u32[]{:S(2)}) copy-start(s32[64]{0:T(128)} %time_ref.1) | copy-start | bytes 772
  38.9 7.9 %copy-start.5 = (s32[64]{0:T(128)S(1)}, s32[64]{0:T(128)}, u32[]{:S(2)}) copy-start(s32[64]{0:T(128)} %length_ref.1) | copy-start | bytes 772
  38.9 7.9 %copy-start.6 = (f32[32]{0:T(128)S(1)}, f32[32]{0:T(128)}, u32[]{:S(2)}) copy-start(f32[32]{0:T(128)} %step_ref.1) | copy-start | bytes 388
  44.8 4.2 %collective-permute-start = (bf16[512,768]{1,0:T(8,128)(2,1)S(1)}, bf16[512,768]{1,0:T(8,128)(2,1)S(1)}, u32[]{:S(2)}, u32[]{:S(2)}) collective-permute-start(bf16[512,768]{1,0:T(8,128)(2,1)S(1)} %bitcast.12), channel_id=1, source_target_pairs={{0,8},{8,0},{1,9},{9,1},{2,10},{10,2},{3,11},{11,3},{4,12},{12,4},... | collective-permute-start | bytes 2359304 | tf_op jit(solution)/shard_map/ppermute | solution.py:153

commit v3 on v2

v3 whole, which is shorter than its diff:
```python
import functools

import jax
import jax.numpy as jnp
from jax import lax
from jax.experimental import pallas as pl
from jax.experimental.pallas import tpu as pltpu
from jax.sharding import Mesh
from jax.sharding import PartitionSpec as P

HD = 128
HEADS = 3
WIDE = HEADS * HD
SETS = 8
BANDS = 4
ORDER = (0, 1, 3, 2)
ROWS = 8
SLOTS = 64
SWAP = [(0, 1), (1, 0)]
LOW = -(2.0**100)
LOG2E = 1.4426950408889634
LIMIT = pltpu.CompilerParams(vmem_limit_bytes=16 * 2**20)


def prepare(
    time_ref, length_ref, step_ref, level_ref, visible_ref, latent_ref, noise_ref, gate_ref,
    bias_ref, base_ref, slope_ref,
):
    band = lax.axis_index("yh")
    core = lax.axis_index("core")
    column = lax.axis_index("yl") * 8 + lax.axis_index("x") * 2 + core
    keys = bias_ref.shape[1]
    groups = visible_ref.shape[0]
    lane = lax.broadcasted_iota(jnp.int32, (1, keys), 1)
    key_set = lane // SLOTS
    key_offset = lane - key_set * SLOTS
    shift = lax.broadcasted_iota(jnp.int32, (BANDS, 1), 0)
    shift = jnp.where(shift < 2, shift, BANDS + 1 - shift)
    own = lax.rem(band + BANDS - shift, BANDS) * (2 * SETS) + column
    pick = own == lax.broadcasted_iota(jnp.int32, (BANDS, groups), 1)
    rows = jnp.dot(
        pick.astype(jnp.bfloat16),
        visible_ref[...].astype(jnp.float32).astype(jnp.bfloat16),
        preferred_element_type=jnp.float32,
    ).astype(jnp.bfloat16)
    for half, key_core in enumerate((core, 1 - core)):
        key_group = band * (2 * SETS) + key_set * 2 + key_core
        length = jnp.zeros((1, keys), jnp.int32)
        for j in range(SETS):
            length = jnp.where(
                key_set == j, length_ref[band * (2 * SETS) + 2 * j + key_core], length
            )
        spread = lax.broadcasted_iota(jnp.int32, (groups, keys), 0) == key_group
        seen = jnp.dot(rows, spread.astype(jnp.bfloat16), preferred_element_type=jnp.float32)
        reach = (key_group == own) | ((key_group < own) & (seen > 0.5))
        bias = jnp.where(reach & (key_offset < length), 0.0, LOW)
        bias_ref[half * BANDS : (half + 1) * BANDS, :] = bias
    group = band * 2 + lax.axis_index("yl")
    group = (group * 4 + lax.axis_index("x")) * 2 + core
    now = time_ref[group]
    offset = lax.axis_index("head") * ROWS + lax.broadcasted_iota(jnp.int32, latent_ref.shape, 0)
    pick = lax.broadcasted_iota(jnp.int32, gate_ref.shape, 0) == now
    gate = jnp.sum(jnp.where(pick, gate_ref[...], 0.0), axis=0, keepdims=True)
    slope_ref[...] = jnp.where(offset < length_ref[group], step_ref[now] * gate, 0.0)
    base_ref[...] = latent_ref[...] + level_ref[now] * noise_ref[...]


def attend(*refs):
    query_refs, key_refs = refs[:BANDS], refs[BANDS : BANDS + 2]
    bias_ref, out_ref = refs[BANDS + 2 :]
    band = lax.axis_index("yh")
    bands = [lax.rem(band + BANDS - k, BANDS) for k in ORDER]
    keys = key_refs[0].shape[0]
    spot = lax.broadcasted_iota(jnp.int32, (SLOTS, HD), 1)
    stats = [jnp.zeros((SLOTS, HD), jnp.float32)] * BANDS
    ones = jnp.ones((keys, HD), jnp.bfloat16)
    for h in range(HEADS):
        part = slice(h * HD, (h + 1) * HD)
        query = jnp.concatenate([q[:, part] for q in query_refs], axis=0)
        scores = [
            lax.dot_general(
                query, key[:, part], (((1,), (1,)), ((), ())), preferred_element_type=jnp.float32
            )
            for key in key_refs
        ]
        raws, tops = ([], []), []
        for k in range(BANDS):
            place = slice(k * SLOTS, (k + 1) * SLOTS)
            score = [
                s[place] * (HD**-0.5 * LOG2E) + bias_ref[half * BANDS + k : half * BANDS + k + 1, :]
                for half, s in enumerate(scores)
            ]
            top = jnp.max(jnp.maximum(*score), axis=1, keepdims=True)
            top = top.astype(jnp.bfloat16).astype(jnp.float32)
            tops.append(top)
            for raw, s in zip(raws, score):
                raw.append(jnp.exp2(s - top).astype(jnp.bfloat16))
        mixed = jnp.zeros((BANDS * SLOTS, 2 * HD), jnp.float32)
        for raw, key in zip(raws, key_refs):
            values = jnp.concatenate([key[:, WIDE + h * HD : WIDE + (h + 1) * HD], ones], axis=1)
            mixed += jnp.dot(
                jnp.concatenate(raw, axis=0), values, preferred_element_type=jnp.float32
            )
        for k in range(BANDS):
            block = mixed[k * SLOTS : (k + 1) * SLOTS]
            out_ref[bands[k], :, part] = block[:, :HD].astype(jnp.bfloat16)
            total = block[:, HD:]
            coarse = total.astype(jnp.bfloat16).astype(jnp.float32)
            stat = stats[k]
            stat = jnp.where(spot == h, tops[k], stat)
            stat = jnp.where(spot == h + 32, coarse, stat)
            stats[k] = jnp.where(spot == h + 64, total - coarse, stat)
    for k in range(BANDS):
        out_ref[bands[k], :, WIDE:] = stats[k].astype(jnp.bfloat16)


def update(part_ref, base_ref, slope_ref, out_ref):
    for g in range(SETS):
        stats = [part_ref[b * SETS + g, :, WIDE:].astype(jnp.float32) for b in range(BANDS)]
        top = functools.reduce(jnp.maximum, stats)
        scale = [jnp.exp2(s - top) for s in stats]
        sums = [pltpu.roll(s, HD - 32, 1) + pltpu.roll(s, HD - 64, 1) for s in stats]
        total = functools.reduce(jnp.add, [w * s for w, s in zip(scale, sums)])
        scale = [w / total for w in scale]
        for h in range(HEADS):
            part = slice(h * HD, (h + 1) * HD)
            mixed = functools.reduce(
                jnp.add,
                [
                    scale[b][:, h : h + 1] * part_ref[b * SETS + g, :, part].astype(jnp.float32)
                    for b in range(BANDS)
                ],
            )
            place = slice((g * HEADS + h) * HD, (g * HEADS + h + 1) * HD)
            out_ref[:, place] = base_ref[:, place] + slope_ref[:, place] * mixed


def local(
    queries,
    key_rows,
    value_rows,
    latent,
    fresh_noise,
    time_index,
    lengths,
    visible,
    time_gate,
    step_size,
    noise_level,
):
    vmem = pl.BlockSpec(memory_space=pltpu.VMEM)
    smem = pl.BlockSpec(memory_space=pltpu.SMEM)
    mine = jnp.concatenate(
        [a.reshape(ROWS, SETS, WIDE).swapaxes(0, 1) for a in (key_rows, value_rows, queries)],
        axis=2,
    )
    mine = lax.all_to_all(mine, "head", split_axis=0, concat_axis=0, tiled=True)
    mine = mine.reshape(SLOTS, 3 * WIDE)
    query = mine[:, 2 * WIDE :]
    own = lax.all_to_all(
        jnp.broadcast_to(mine[None, :, : 2 * WIDE], (SETS, SLOTS, 2 * WIDE)),
        ("yl", "x"),
        split_axis=0,
        concat_axis=0,
        tiled=True,
    ).reshape(SETS * SLOTS, 2 * WIDE)
    sent = [
        lax.ppermute(query, "yh", [(i, (i + k) % BANDS) for i in range(BANDS)])
        for k in ORDER[1:]
    ]
    bias = jax.ShapeDtypeStruct((2 * BANDS, SETS * SLOTS), jnp.float32)
    prepared = pl.pallas_call(
        prepare,
        out_shape=[bias] + [jax.ShapeDtypeStruct(latent.shape, jnp.float32)] * 2,
        in_specs=[smem] * 4 + [vmem] * 4,
        out_specs=[vmem] * 3,
        compiler_params=LIMIT,
    )(time_index, lengths, step_size, noise_level, visible, latent, fresh_noise, time_gate)
    own, sent = lax.optimization_barrier((own, sent))
    bias, base, slope = prepared
    other = lax.ppermute(own, "core", SWAP)
    partial = pl.pallas_call(
        attend,
        out_shape=jax.ShapeDtypeStruct((BANDS, SLOTS, WIDE + HD), jnp.bfloat16),
        in_specs=[vmem] * (BANDS + 3),
        out_specs=vmem,
        compiler_params=LIMIT,
    )(query, *sent, own, other, bias)
    partial = lax.all_to_all(
        partial.reshape(BANDS * SETS, ROWS, WIDE + HD),
        ("yh", "head"),
        split_axis=0,
        concat_axis=0,
        tiled=True,
    )
    return pl.pallas_call(
        update,
        out_shape=jax.ShapeDtypeStruct(latent.shape, jnp.float32),
        in_specs=[vmem] * 3,
        out_specs=vmem,
        compiler_params=LIMIT,
    )(partial, base, slope)


def solution(mesh):
    names = ("yh", "yl", "x", "core", "head")
    grid = Mesh(mesh.devices.reshape(BANDS, 2, 4, 2, 8), names)
    tokens = P(names, None)
    placed = (tokens,) * 5 + (P(),) * 6
    return jax.shard_map(local, mesh=grid, in_specs=placed, out_specs=tokens, check_vma=False)
```

time: 72.6 us -> 72.2 us (level)
  the two profiles are of different devices: /device:TPU:8 before, /device:TPU:10 now
where the time goes in v3:
time: 72.2 us; the launch traced here: 71.7 us
  blocking collectives  38.4 us (53%)
  starting transfers between devices  21.5 us (30%)
  waiting for transfers between devices  6.35 us (9%)
  Pallas kernels  3.44 us (5%)
  local copies, waits for them, and re-layouts  1.02 us (1%)
  other arithmetic  0.86 us (1%)
    all_to_all x1, blocking collectives, local(): mine = lax.all_to_all(mine, 'head', split_axis=0, concat_axis=0, tiled=True)  19.5 us
    all_to_all x1, blocking collectives, local(): lax.all_to_all(partial.reshape(BANDS * SETS, ROWS, WIDE + HD), ('yh', 'he...  18.9 us
    ppermute x3, starting transfers between devices, local(): lax.ppermute(query, 'yh', [(i, (i + k) % BANDS) for i in range(BANDS)])  13.7 us
    all_to_all x1, starting transfers between devices, local(): lax.all_to_all(jnp.broadcast_to(mine[None, :, :2 * WIDE], (SETS, SLOTS, 2...  5.87 us
    ppermute x3, waiting for transfers between devices, local(): lax.ppermute(query, 'yh', [(i, (i + k) % BANDS) for i in range(BANDS)])  5.01 us
    ppermute x1, starting transfers between devices, local(): other = lax.ppermute(own, 'core', SWAP)  1.91 us
  transfers between devices with their start and end apart: 5, of which 3 were waited for; matrix products, arithmetic and copies ran while one was open for 0% of the time, Pallas kernels for 1%

profile of v3, /device:TPU:10, one launch (start us, length us, event | category | flops | bytes accessed | tf_op | source)
XLA Modules:
  0.0 71.7 jit_solution(9346277067969013035)
XLA Ops:
  0.0 0.9 %pad_maximum_fusion = bf16[8,8,1152]{2,1,0:T(8,128)(2,1)S(1)} fusion(bf16[8,8,384]{2,1,0:T(8,128)(2,1)} %bitcast.17, bf16[8,8,384]{2,1,0:T(8,128)(2,1)} %bitcast.18, bf16[8,8,384]{2,1,0:T(8,128)(2,1)} %bitcast.19), kind=kLoop, calls=%fused_computation | loop fusion | flops 442368 | bytes 294912 | tf_op jit(solution)/shard_map/concatenate | solution.py:153
  0.9 19.5 %all_to_all.15 = bf16[8,8,1152]{2,1,0:T(8,128)(2,1)S(1)} all-to-all(bf16[8,8,1152]{2,1,0:T(8,128)(2,1)S(1)} %pad_maximum_fusion), channel_id=1, replica_groups=mesh['yh'=4,'yl'=2,'x'=4,'core'=2,'head'=8] {'head'}, dimensions={0} | all-to-all | bytes 294912 | tf_op jit(solution)/shard_map/all_to_all | solution.py:157
  20.4 1.0 %broadcast_in_dim.2 = bf16[8,64,768]{2,1,0:T(8,128)(2,1)} broadcast(bf16[64,768]{1,0:T(8,128)(2,1)S(1)} %slice.9), dimensions={1,2} | broadcast | bytes 884736 | tf_op jit(solution)/shard_map/broadcast_in_dim | solution.py:161
  21.4 0.0 copy-start
  21.4 0.0 copy-start.2
  21.4 0.0 copy-start.3
  21.4 0.0 copy-start.7
  21.4 5.9 %all-to-all-start.1 = ((bf16[8,64,768]{2,1,0:T(8,128)(2,1)}), bf16[8,64,768]{2,1,0:T(8,128)(2,1)S(1)}, u32[]{:S(2)}, u32[]{:S(2)}) async-start(bf16[8,64,768]{2,1,0:T(8,128)(2,1)} %broadcast_in_dim.2), calls=%async_computation.1 | async-start | bytes 1572864 | tf_op jit(solution)/shard_map/all_to_all | solution.py:160
  27.3 0.0 copy-start.4
  27.3 0.0 copy-start.5
  27.3 0.0 copy-start.6
  27.3 7.0 %collective-permute-start.2 = (bf16[64,384]{1,0:T(8,128)(2,1)S(1)}, bf16[64,384]{1,0:T(8,128)(2,1)S(1)}, u32[]{:S(2)}, u32[]{:S(2)}) collective-permute-start(bf16[64,384]{1,0:T(8,128)(2,1)S(1)} %slice.8.refs_0_), channel_id=1, source_target_pairs={{0,256},{128,384},{256,0},{384,128},{1,257},{129,385},{257,1},{385... | collective-permute-start | bytes 147464 | tf_op jit(solution)/shard_map/ppermute | solution.py:168
  34.3 3.1 %collective-permute-start.1 = (bf16[64,384]{1,0:T(8,128)(2,1)S(1)}, bf16[64,384]{1,0:T(8,128)(2,1)S(1)}, u32[]{:S(2)}, u32[]{:S(2)}) collective-permute-start(bf16[64,384]{1,0:T(8,128)(2,1)S(1)} %slice.8.refs_0_), channel_id=1, source_target_pairs={{0,384},{128,0},{256,128},{384,256},{1,385},{129,1},{257,129},{385... | collective-permute-start | bytes 147464 | tf_op jit(solution)/shard_map/ppermute | solution.py:168
  37.4 3.6 %collective-permute-start = (bf16[64,384]{1,0:T(8,128)(2,1)S(1)}, bf16[64,384]{1,0:T(8,128)(2,1)S(1)}, u32[]{:S(2)}, u32[]{:S(2)}) collective-permute-start(bf16[64,384]{1,0:T(8,128)(2,1)S(1)} %slice.8.refs_0_), channel_id=1, source_target_pairs={{0,128},{128,256},{256,384},{384,0},{1,129},{129,257},{257,385},{3... | collective-permute-start | bytes 147464 | tf_op jit(solution)/shard_map/ppermute | solution.py:168
  41.0 1.9 %collective-permute-done.2.refs_3_ = bf16[64,384]{1,0:T(8,128)(2,1)S(1)} collective-permute-done((bf16[64,384]{1,0:T(8,128)(2,1)S(1)}, bf16[64,384]{1,0:T(8,128)(2,1)S(1)}, u32[]{:S(2)}, u32[]{:S(2)}) %collective-permute-start.2) | collective-permute-done | bytes 49184 | tf_op jit(solution)/shard_map/ppermute | solution.py:168
  42.9 0.0 collective-permute-done.1.refs_2_
  42.9 3.1 %collective-permute-done.refs_1_ = bf16[64,384]{1,0:T(8,128)(2,1)S(1)} collective-permute-done((bf16[64,384]{1,0:T(8,128)(2,1)S(1)}, bf16[64,384]{1,0:T(8,128)(2,1)S(1)}, u32[]{:S(2)}, u32[]{:S(2)}) %collective-permute-start) | collective-permute-done | bytes 49184 | tf_op jit(solution)/shard_map/ppermute | solution.py:168
  46.1 0.0 all-to-all-done.1
  46.1 1.9 %collective-permute-start.3 = (bf16[512,768]{1,0:T(8,128)(2,1)S(1)}, bf16[512,768]{1,0:T(8,128)(2,1)S(1)}, u32[]{:S(2)}, u32[]{:S(2)}) collective-permute-start(bf16[512,768]{1,0:T(8,128)(2,1)S(1)} %bitcast.12), channel_id=1, source_target_pairs={{0,8},{8,0},{1,9},{9,1},{2,10},{10,2},{3,11},{11,3},{4,12},{12,4},... | collective-permute-start | bytes 2359304 | tf_op jit(solution)/shard_map/ppermute | solution.py:181
  48.0 0.0 copy-done
  48.0 0.0 copy-done.2
  48.0 0.0 copy-done.3
  48.0 0.0 copy-done.7
  48.0 0.0 copy-done.1
  48.0 0.0 copy-done.4
  48.0 0.0 copy-done.5
  48.0 0.0 copy-done.6
  48.1 0.8 %shard_map.109 = (f32[8,512]{1,0:T(8,128)S(1)}, f32[8,3072]{1,0:T(8,128)S(1)}, f32[8,3072]{1,0:T(8,128)S(1)}) custom-call(s32[64]{0:T(128)S(1)} %copy-done.4, s32[64]{0:T(128)S(1)} %copy-done.5, f32[32]{0:T(128)S(1)} %copy-done.6, f32[32]{0:T(128)S(1)} %copy-done.7, s32[64,64]{1,0:T(8,128)S(1)} %copy-done.3, f32[8,3072]{1,0:T(8,128)S(1)} %copy-done.1, ...), custom_call_target="tpu_custom_call" | custom-call | tf_op jit(solution)/shard_map/pallas_call | solution.py:172
  48.9 1.3 %collective-permute-done.3.refs_5_ = bf16[512,768]{1,0:T(8,128)(2,1)S(1)} collective-permute-done((bf16[512,768]{1,0:T(8,128)(2,1)S(1)}, bf16[512,768]{1,0:T(8,128)(2,1)S(1)}, u32[]{:S(2)}, u32[]{:S(2)}) %collective-permute-start.3) | collective-permute-done | bytes 786464 | tf_op jit(solution)/shard_map/ppermute | solution.py:181
  50.2 1.4 %shard_map.110 = bf16[4,64,512]{2,1,0:T(8,128)(2,1)S(1)} custom-call(bf16[64,384]{1,0:T(8,128)(2,1)S(1)} %slice.8.refs_0_, bf16[64,384]{1,0:T(8,128)(2,1)S(1)} %collective-permute-done.refs_1_, bf16[64,384]{1,0:T(8,128)(2,1)S(1)} %collective-permute-done.1.refs_2_, bf16[64,384]{1,0:T(8,128)(2,1)S(1)} %collective-permute-done.2.refs_3_, ...), custom_call_target="tpu_custom_call" | custom-call | tf_op jit(solution)/shard_map/pallas_call | solution.py:182
  51.7 18.9 %all_to_all.16.part_ref = bf16[32,8,512]{2,1,0:T(8,128)(2,1)S(1)} all-to-all(bf16[32,8,512]{2,1,0:T(8,128)(2,1)S(1)} %bitcast.14), channel_id=1, replica_groups=mesh['yh'=4,'yl'=2,'x'=4,'core'=2,'head'=8] {'yh','head'}, dimensions={0} | all-to-all | bytes 524288 | tf_op jit(solution)/shard_map/all_to_all | solution.py:189
  70.6 1.2 %shard_map.111 = f32[8,3072]{1,0:T(8,128)} custom-call(bf16[32,8,512]{2,1,0:T(8,128)(2,1)S(1)} %all_to_all.16.part_ref, f32[8,3072]{1,0:T(8,128)S(1)} %get-tuple-element.17.base_ref, f32[8,3072]{1,0:T(8,128)S(1)} %get-tuple-element.18.slope_ref), custom_call_target="tpu_custom_call" | custom-call | tf_op jit(solution)/shard_map/pallas_call | solution.py:196
  (3 shorter events, 0.0 us)
Async XLA Ops:
  21.4 26.6 %copy-start = (f32[32,3072]{1,0:T(8,128)S(1)}, f32[32,3072]{1,0:T(8,128)}, u32[]{:S(2)}) copy-start(f32[32,3072]{1,0:T(8,128)} %gate_ref.1) | copy-start | bytes 1179652
  21.4 26.6 %copy-start.2 = (f32[8,3072]{1,0:T(8,128)S(1)}, f32[8,3072]{1,0:T(8,128)}, u32[]{:S(2)}) copy-start(f32[8,3072]{1,0:T(8,128)} %noise_ref.1) | copy-start | bytes 294916
  21.4 26.6 %copy-start.3 = (s32[64,64]{1,0:T(8,128)S(1)}, s32[64,64]{1,0:T(8,128)}, u32[]{:S(2)}) copy-start(s32[64,64]{1,0:T(8,128)} %visible_ref.1) | copy-start | bytes 49156
  21.4 26.6 %copy-start.7 = (f32[32]{0:T(128)S(1)}, f32[32]{0:T(128)}, u32[]{:S(2)}) copy-start(f32[32]{0:T(128)} %level_ref.1) | copy-start | bytes 388
  21.4 24.7 %all-to-all-start.1 = ((bf16[8,64,768]{2,1,0:T(8,128)(2,1)}), bf16[8,64,768]{2,1,0:T(8,128)(2,1)S(1)}, u32[]{:S(2)}, u32[]{:S(2)}) async-start(bf16[8,64,768]{2,1,0:T(8,128)(2,1)} %broadcast_in_dim.2), calls=%async_computation.1 | async-start | bytes 1572864 | tf_op jit(solution)/shard_map/all_to_all | solution.py:160
  27.3 20.8 %copy-start.1 = (f32[8,3072]{1,0:T(8,128)S(1)}, f32[8,3072]{1,0:T(8,128)}, u32[]{:S(2)}) copy-start(f32[8,3072]{1,0:T(8,128)} %latent_ref.1) | copy-start | bytes 294916
  27.3 20.8 %copy-start.4 = (s32[64]{0:T(128)S(1)}, s32[64]{0:T(128)}, u32[]{:S(2)}) copy-start(s32[64]{0:T(128)} %time_ref.1) | copy-start | bytes 772
  27.3 20.8 %copy-start.5 = (s32[64]{0:T(128)S(1)}, s32[64]{0:T(128)}, u32[]{:S(2)}) copy-start(s32[64]{0:T(128)} %length_ref.1) | copy-start | bytes 772
  27.3 20.7 %copy-start.6 = (f32[32]{0:T(128)S(1)}, f32[32]{0:T(128)}, u32[]{:S(2)}) copy-start(f32[32]{0:T(128)} %step_ref.1) | copy-start | bytes 388
  27.3 15.6 %collective-permute-start.2 = (bf16[64,384]{1,0:T(8,128)(2,1)S(1)}, bf16[64,384]{1,0:T(8,128)(2,1)S(1)}, u32[]{:S(2)}, u32[]{:S(2)}) collective-permute-start(bf16[64,384]{1,0:T(8,128)(2,1)S(1)} %slice.8.refs_0_), channel_id=1, source_target_pairs={{0,256},{128,384},{256,0},{384,128},{1,257},{129,385},{257,1},{385... | collective-permute-start | bytes 147464 | tf_op jit(solution)/shard_map/ppermute | solution.py:168
  34.3 8.6 %collective-permute-start.1 = (bf16[64,384]{1,0:T(8,128)(2,1)S(1)}, bf16[64,384]{1,0:T(8,128)(2,1)S(1)}, u32[]{:S(2)}, u32[]{:S(2)}) collective-permute-start(bf16[64,384]{1,0:T(8,128)(2,1)S(1)} %slice.8.refs_0_), channel_id=1, source_target_pairs={{0,384},{128,0},{256,128},{384,256},{1,385},{129,1},{257,129},{385... | collective-permute-start | bytes 147464 | tf_op jit(solution)/shard_map/ppermute | solution.py:168
  37.4 8.6 %collective-permute-start = (bf16[64,384]{1,0:T(8,128)(2,1)S(1)}, bf16[64,384]{1,0:T(8,128)(2,1)S(1)}, u32[]{:S(2)}, u32[]{:S(2)}) collective-permute-start(bf16[64,384]{1,0:T(8,128)(2,1)S(1)} %slice.8.refs_0_), channel_id=1, source_target_pairs={{0,128},{128,256},{256,384},{384,0},{1,129},{129,257},{257,385},{3... | collective-permute-start | bytes 147464 | tf_op jit(solution)/shard_map/ppermute | solution.py:168
  46.1 4.2 %collective-permute-start.3 = (bf16[512,768]{1,0:T(8,128)(2,1)S(1)}, bf16[512,768]{1,0:T(8,128)(2,1)S(1)}, u32[]{:S(2)}, u32[]{:S(2)}) collective-permute-start(bf16[512,768]{1,0:T(8,128)(2,1)S(1)} %bitcast.12), channel_id=1, source_target_pairs={{0,8},{8,0},{1,9},{9,1},{2,10},{10,2},{3,11},{11,3},{4,12},{12,4},... | collective-permute-start | bytes 2359304 | tf_op jit(solution)/shard_map/ppermute | solution.py:181

commit v4 on v3

--- a/solution.py
+++ b/solution.py
@@ -13,7 +13,7 @@
 WIDE = HEADS * HD
 SETS = 8
 BANDS = 4
-ORDER = (0, 1, 3, 2)
+ORDER = (0, 2, 1, 3)
 ROWS = 8
 SLOTS = 64
 SWAP = [(0, 1), (1, 0)]
@@ -35,7 +35,7 @@
     key_set = lane // SLOTS
     key_offset = lane - key_set * SLOTS
     shift = lax.broadcasted_iota(jnp.int32, (BANDS, 1), 0)
-    shift = jnp.where(shift < 2, shift, BANDS + 1 - shift)
+    shift = sum(jnp.where(shift == k, ORDER[k], 0) for k in range(BANDS))
     own = lax.rem(band + BANDS - shift, BANDS) * (2 * SETS) + column
     pick = own == lax.broadcasted_iota(jnp.int32, (BANDS, groups), 1)
     rows = jnp.dot(
@@ -43,12 +43,14 @@
         visible_ref[...].astype(jnp.float32).astype(jnp.bfloat16),
         preferred_element_type=jnp.float32,
     ).astype(jnp.bfloat16)
-    for half, key_core in enumerate((core, 1 - core)):
-        key_group = band * (2 * SETS) + key_set * 2 + key_core
+    for half in range(2):
+        local_group = (lane // SLOTS % BANDS + half * BANDS) * 2 + lane // (SLOTS * BANDS)
+        key_group = band * (2 * SETS) + local_group
         length = jnp.zeros((1, keys), jnp.int32)
         for j in range(SETS):
+            local = half * SETS + j
             length = jnp.where(
-                key_set == j, length_ref[band * (2 * SETS) + 2 * j + key_core], length
+                local_group == local, length_ref[band * (2 * SETS) + local], length
             )
         spread = lax.broadcasted_iota(jnp.int32, (groups, keys), 0) == key_group
         seen = jnp.dot(rows, spread.astype(jnp.bfloat16), preferred_element_type=jnp.float32)
@@ -163,7 +165,7 @@
         split_axis=0,
         concat_axis=0,
         tiled=True,
-    ).reshape(SETS * SLOTS, 2 * WIDE)
+    )
     sent = [
         lax.ppermute(query, "yh", [(i, (i + k) % BANDS) for i in range(BANDS)])
         for k in ORDER[1:]
@@ -176,16 +178,18 @@
         out_specs=[vmem] * 3,
         compiler_params=LIMIT,
     )(time_index, lengths, step_size, noise_level, visible, latent, fresh_noise, time_gate)
-    own, sent = lax.optimization_barrier((own, sent))
     bias, base, slope = prepared
-    other = lax.ppermute(own, "core", SWAP)
+    halves = [
+        lax.all_gather(a.reshape(-1, 2 * WIDE), "core", axis=0, tiled=True)
+        for a in (own[:BANDS], own[BANDS:])
+    ]
     partial = pl.pallas_call(
         attend,
         out_shape=jax.ShapeDtypeStruct((BANDS, SLOTS, WIDE + HD), jnp.bfloat16),
         in_specs=[vmem] * (BANDS + 3),
         out_specs=vmem,
         compiler_params=LIMIT,
-    )(query, *sent, own, other, bias)
+    )(query, *sent, *halves, bias)
     partial = lax.all_to_all(
         partial.reshape(BANDS * SETS, ROWS, WIDE + HD),
         ("yh", "head"),

time: 72.2 us -> 68.6 us (0.950)
  waiting for transfers between devices: 6.35 us -> 0.01 us
  blocking collectives: 38.4 us -> 42 us
  starting transfers between devices: 21.5 us -> 20.7 us
    ppermute x3, waiting for transfers between devices: 5.01 us -> 0.01 us  [local(): lax.ppermute(query, 'yh', [(i, (i + k) % BANDS) for i in range(BANDS)])]
    all_gather x0 -> x2, blocking collectives: none -> 4.73 us  [local(): lax.all_gather(a.reshape(-1, 2 * WIDE), 'core', axis=0, tiled=True)]
    ppermute x1 -> x0, starting transfers between devices: 1.91 us -> none  [local(): other = lax.ppermute(own, 'core', SWAP)]
    ppermute x1 -> x0, waiting for transfers between devices: 1.34 us -> none  [local(): other = lax.ppermute(own, 'core', SWAP)]
    all_to_all x1, blocking collectives: 18.9 us -> 17.7 us  [local(): lax.all_to_all(partial.reshape(BANDS * SETS, ROWS, WIDE + HD), ('yh', 'he...]
    ppermute x3, starting transfers between devices: 13.7 us -> 14.8 us  [local(): lax.ppermute(query, 'yh', [(i, (i + k) % BANDS) for i in range(BANDS)])]
  transfers between devices with their start and end apart: 5 -> 4, of which waited for: 3 -> 0; matrix products, arithmetic and copies ran while one was open for 0% -> 0% of each run, Pallas kernels for 1% -> 1%
where the time goes in v4:
time: 68.6 us; the launch traced here: 68.2 us
  blocking collectives  42 us (61%)
  starting transfers between devices  20.7 us (30%)
  Pallas kernels  3.44 us (5%)
  local copies, waits for them, and re-layouts  1.08 us (2%)
  other arithmetic  0.86 us (1%)
    all_to_all x1, blocking collectives, local(): mine = lax.all_to_all(mine, 'head', split_axis=0, concat_axis=0, tiled=True)  19.5 us
    all_to_all x1, blocking collectives, local(): lax.all_to_all(partial.reshape(BANDS * SETS, ROWS, WIDE + HD), ('yh', 'he...  17.7 us
    ppermute x3, starting transfers between devices, local(): lax.ppermute(query, 'yh', [(i, (i + k) % BANDS) for i in range(BANDS)])  14.8 us
    all_to_all x1, starting transfers between devices, local(): lax.all_to_all(jnp.broadcast_to(mine[None, :, :2 * WIDE], (SETS, SLOTS, 2...  5.87 us
    all_gather x2, blocking collectives, local(): lax.all_gather(a.reshape(-1, 2 * WIDE), 'core', axis=0, tiled=True)  4.73 us
    pallas_call x1, Pallas kernels, local(): pl.pallas_call(attend, out_shape=jax.ShapeDtypeStruct((BANDS, SLOTS, WIDE...  1.45 us
  transfers between devices with their start and end apart: 4, of which 0 were waited for; matrix products, arithmetic and copies ran while one was open for 0% of the time, Pallas kernels for 1%

profile of v4, /device:TPU:10, one launch (start us, length us, event | category | flops | bytes accessed | tf_op | source)
XLA Modules:
  0.0 68.2 jit_solution(2650420698401230777)
XLA Ops:
  0.0 0.9 %pad_maximum_fusion = bf16[8,8,1152]{2,1,0:T(8,128)(2,1)S(1)} fusion(bf16[8,8,384]{2,1,0:T(8,128)(2,1)} %bitcast.18, bf16[8,8,384]{2,1,0:T(8,128)(2,1)} %bitcast.19, bf16[8,8,384]{2,1,0:T(8,128)(2,1)} %bitcast.20), kind=kLoop, calls=%fused_computation | loop fusion | flops 442368 | bytes 294912 | tf_op jit(solution)/shard_map/concatenate | solution.py:155
  0.9 19.5 %all_to_all.15 = bf16[8,8,1152]{2,1,0:T(8,128)(2,1)S(1)} all-to-all(bf16[8,8,1152]{2,1,0:T(8,128)(2,1)S(1)} %pad_maximum_fusion), channel_id=1, replica_groups=mesh['yh'=4,'yl'=2,'x'=4,'core'=2,'head'=8] {'head'}, dimensions={0} | all-to-all | bytes 294912 | tf_op jit(solution)/shard_map/all_to_all | solution.py:159
  20.4 1.0 %broadcast_in_dim.2 = bf16[8,64,768]{2,1,0:T(8,128)(2,1)} broadcast(bf16[64,768]{1,0:T(8,128)(2,1)S(1)} %slice.17), dimensions={1,2} | broadcast | bytes 884736 | tf_op jit(solution)/shard_map/broadcast_in_dim | solution.py:163
  21.4 0.0 copy-start
  21.4 0.0 copy-start.1
  21.4 0.0 copy-start.4
  21.4 0.0 copy-start.5
  21.4 0.0 copy-start.6
  21.4 0.0 copy-start.7
  21.4 5.9 %all-to-all-start.1 = ((bf16[8,64,768]{2,1,0:T(8,128)(2,1)}), bf16[8,64,768]{2,1,0:T(8,128)(2,1)S(1)}, u32[]{:S(2)}, u32[]{:S(2)}) async-start(bf16[8,64,768]{2,1,0:T(8,128)(2,1)} %broadcast_in_dim.2), calls=%async_computation.1 | async-start | bytes 1572864 | tf_op jit(solution)/shard_map/all_to_all | solution.py:162
  27.3 0.0 copy-done
  27.3 0.0 copy-done.1
  27.3 0.0 copy-done.2
  27.3 0.0 copy-done.3
  27.3 0.0 copy-done.4
  27.3 0.0 copy-done.5
  27.4 0.0 copy-done.6
  27.4 0.0 copy-done.7
  27.4 0.8 %shard_map.109 = (f32[8,512]{1,0:T(8,128)S(1)}, f32[8,3072]{1,0:T(8,128)S(1)}, f32[8,3072]{1,0:T(8,128)S(1)}) custom-call(s32[64]{0:T(128)S(1)} %copy-done.4, s32[64]{0:T(128)S(1)} %copy-done.5, f32[32]{0:T(128)S(1)} %copy-done.6, f32[32]{0:T(128)S(1)} %copy-done.7, s32[64,64]{1,0:T(8,128)S(1)} %copy-done.3, f32[8,3072]{1,0:T(8,128)S(1)} %copy-done.1, ...), custom_call_target="tpu_custom_call" | custom-call | tf_op jit(solution)/shard_map/pallas_call | solution.py:174
  28.2 6.8 %collective-permute-start = (bf16[64,384]{1,0:T(8,128)(2,1)S(1)}, bf16[64,384]{1,0:T(8,128)(2,1)S(1)}, u32[]{:S(2)}, u32[]{:S(2)}) collective-permute-start(bf16[64,384]{1,0:T(8,128)(2,1)S(1)} %slice.16.refs_0_), channel_id=1, source_target_pairs={{0,256},{128,384},{256,0},{384,128},{1,257},{129,385},{257,1},{385... | collective-permute-start | bytes 147464 | tf_op jit(solution)/shard_map/ppermute | solution.py:170
  35.1 2.7 %collective-permute-start.1 = (bf16[64,384]{1,0:T(8,128)(2,1)S(1)}, bf16[64,384]{1,0:T(8,128)(2,1)S(1)}, u32[]{:S(2)}, u32[]{:S(2)}) collective-permute-start(bf16[64,384]{1,0:T(8,128)(2,1)S(1)} %slice.16.refs_0_), channel_id=1, source_target_pairs={{0,128},{128,256},{256,384},{384,0},{1,129},{129,257},{257,385},{3... | collective-permute-start | bytes 147464 | tf_op jit(solution)/shard_map/ppermute | solution.py:170
  37.8 5.3 %collective-permute-start.2 = (bf16[64,384]{1,0:T(8,128)(2,1)S(1)}, bf16[64,384]{1,0:T(8,128)(2,1)S(1)}, u32[]{:S(2)}, u32[]{:S(2)}) collective-permute-start(bf16[64,384]{1,0:T(8,128)(2,1)S(1)} %slice.16.refs_0_), channel_id=1, source_target_pairs={{0,384},{128,0},{256,128},{384,256},{1,385},{129,1},{257,129},{385... | collective-permute-start | bytes 147464 | tf_op jit(solution)/shard_map/ppermute | solution.py:170
  43.0 0.0 all-to-all-done.1
  43.0 0.1 fusion
  43.1 2.4 %all_gather.6.refs_4_ = bf16[512,768]{1,0:T(8,128)(2,1)S(1)} all-gather(bf16[256,768]{1,0:T(8,128)(2,1)S(1)} %bitcast.15), channel_id=1, replica_groups=mesh['yh'=4,'yl'=2,'x'=4,'core'=2,'head'=8] {'core'}, dimensions={0}, use_global_device_ids=true | all-gather | bytes 1179648 | tf_op jit(solution)/shard_map/all_gather | solution.py:183
  45.5 2.4 %all_gather.7.refs_5_ = bf16[512,768]{1,0:T(8,128)(2,1)S(1)} all-gather(bf16[256,768]{1,0:T(8,128)(2,1)S(1)} %bitcast.14), channel_id=1, replica_groups=mesh['yh'=4,'yl'=2,'x'=4,'core'=2,'head'=8] {'core'}, dimensions={0}, use_global_device_ids=true | all-gather | bytes 1179648 | tf_op jit(solution)/shard_map/all_gather | solution.py:183
  47.8 0.0 collective-permute-done.refs_1_
  47.8 0.0 collective-permute-done.1.refs_2_
  47.8 0.0 collective-permute-done.2.refs_3_
  47.8 1.4 %shard_map.110 = bf16[4,64,512]{2,1,0:T(8,128)(2,1)S(1)} custom-call(bf16[64,384]{1,0:T(8,128)(2,1)S(1)} %slice.16.refs_0_, bf16[64,384]{1,0:T(8,128)(2,1)S(1)} %collective-permute-done.refs_1_, bf16[64,384]{1,0:T(8,128)(2,1)S(1)} %collective-permute-done.1.refs_2_, bf16[64,384]{1,0:T(8,128)(2,1)S(1)} %collective-permute-done.2.refs_3_, ...), custom_call_target="tpu_custom_call" | custom-call | tf_op jit(solution)/shard_map/pallas_call | solution.py:186
  49.3 17.7 %all_to_all.16.part_ref = bf16[32,8,512]{2,1,0:T(8,128)(2,1)S(1)} all-to-all(bf16[32,8,512]{2,1,0:T(8,128)(2,1)S(1)} %bitcast.13), channel_id=1, replica_groups=mesh['yh'=4,'yl'=2,'x'=4,'core'=2,'head'=8] {'yh','head'}, dimensions={0} | all-to-all | bytes 524288 | tf_op jit(solution)/shard_map/all_to_all | solution.py:193
  67.0 1.2 %shard_map.111 = f32[8,3072]{1,0:T(8,128)} custom-call(bf16[32,8,512]{2,1,0:T(8,128)(2,1)S(1)} %all_to_all.16.part_ref, f32[8,3072]{1,0:T(8,128)S(1)} %get-tuple-element.9.base_ref, f32[8,3072]{1,0:T(8,128)S(1)} %get-tuple-element.10.slope_ref), custom_call_target="tpu_custom_call" | custom-call | tf_op jit(solution)/shard_map/pallas_call | solution.py:200
  (4 shorter events, 0.0 us)
Async XLA Ops:
  21.4 5.9 %copy-start = (f32[32,3072]{1,0:T(8,128)S(1)}, f32[32,3072]{1,0:T(8,128)}, u32[]{:S(2)}) copy-start(f32[32,3072]{1,0:T(8,128)} %gate_ref.1) | copy-start | bytes 1179652
  21.4 5.9 %copy-start.1 = (f32[8,3072]{1,0:T(8,128)S(1)}, f32[8,3072]{1,0:T(8,128)}, u32[]{:S(2)}) copy-start(f32[8,3072]{1,0:T(8,128)} %latent_ref.1) | copy-start | bytes 294916
  21.4 5.9 %copy-start.2 = (f32[8,3072]{1,0:T(8,128)S(1)}, f32[8,3072]{1,0:T(8,128)}, u32[]{:S(2)}) copy-start(f32[8,3072]{1,0:T(8,128)} %noise_ref.1) | copy-start | bytes 294916
  21.4 5.9 %copy-start.3 = (s32[64,64]{1,0:T(8,128)S(1)}, s32[64,64]{1,0:T(8,128)}, u32[]{:S(2)}) copy-start(s32[64,64]{1,0:T(8,128)} %visible_ref.1) | copy-start | bytes 49156
  21.4 6.0 %copy-start.4 = (s32[64]{0:T(128)S(1)}, s32[64]{0:T(128)}, u32[]{:S(2)}) copy-start(s32[64]{0:T(128)} %time_ref.1) | copy-start | bytes 772
  21.4 6.0 %copy-start.5 = (s32[64]{0:T(128)S(1)}, s32[64]{0:T(128)}, u32[]{:S(2)}) copy-start(s32[64]{0:T(128)} %length_ref.1) | copy-start | bytes 772
  21.4 5.9 %copy-start.6 = (f32[32]{0:T(128)S(1)}, f32[32]{0:T(128)}, u32[]{:S(2)}) copy-start(f32[32]{0:T(128)} %step_ref.1) | copy-start | bytes 388
  21.4 5.9 %copy-start.7 = (f32[32]{0:T(128)S(1)}, f32[32]{0:T(128)}, u32[]{:S(2)}) copy-start(f32[32]{0:T(128)} %level_ref.1) | copy-start | bytes 388
  21.4 21.6 %all-to-all-start.1 = ((bf16[8,64,768]{2,1,0:T(8,128)(2,1)}), bf16[8,64,768]{2,1,0:T(8,128)(2,1)S(1)}, u32[]{:S(2)}, u32[]{:S(2)}) async-start(bf16[8,64,768]{2,1,0:T(8,128)(2,1)} %broadcast_in_dim.2), calls=%async_computation.1 | async-start | bytes 1572864 | tf_op jit(solution)/shard_map/all_to_all | solution.py:162
  28.2 19.6 %collective-permute-start = (bf16[64,384]{1,0:T(8,128)(2,1)S(1)}, bf16[64,384]{1,0:T(8,128)(2,1)S(1)}, u32[]{:S(2)}, u32[]{:S(2)}) collective-permute-start(bf16[64,384]{1,0:T(8,128)(2,1)S(1)} %slice.16.refs_0_), channel_id=1, source_target_pairs={{0,256},{128,384},{256,0},{384,128},{1,257},{129,385},{257,1},{385... | collective-permute-start | bytes 147464 | tf_op jit(solution)/shard_map/ppermute | solution.py:170
  35.1 12.8 %collective-permute-start.1 = (bf16[64,384]{1,0:T(8,128)(2,1)S(1)}, bf16[64,384]{1,0:T(8,128)(2,1)S(1)}, u32[]{:S(2)}, u32[]{:S(2)}) collective-permute-start(bf16[64,384]{1,0:T(8,128)(2,1)S(1)} %slice.16.refs_0_), channel_id=1, source_target_pairs={{0,128},{128,256},{256,384},{384,0},{1,129},{129,257},{257,385},{3... | collective-permute-start | bytes 147464 | tf_op jit(solution)/shard_map/ppermute | solution.py:170
  37.8 10.1 %collective-permute-start.2 = (bf16[64,384]{1,0:T(8,128)(2,1)S(1)}, bf16[64,384]{1,0:T(8,128)(2,1)S(1)}, u32[]{:S(2)}, u32[]{:S(2)}) collective-permute-start(bf16[64,384]{1,0:T(8,128)(2,1)S(1)} %slice.16.refs_0_), channel_id=1, source_target_pairs={{0,384},{128,0},{256,128},{384,256},{1,385},{129,1},{257,129},{385... | collective-permute-start | bytes 147464 | tf_op jit(solution)/shard_map/ppermute | solution.py:170

commit v5 on v4

--- a/solution.py
+++ b/solution.py
@@ -44,14 +44,16 @@
         preferred_element_type=jnp.float32,
     ).astype(jnp.bfloat16)
     for half in range(2):
-        local_group = (lane // SLOTS % BANDS + half * BANDS) * 2 + lane // (SLOTS * BANDS)
+        key_set = lane // SLOTS % BANDS + half * BANDS
+        local_group = key_set % 2 * SETS + key_set // 2 * 2 + lane // (SLOTS * BANDS)
         key_group = band * (2 * SETS) + local_group
         length = jnp.zeros((1, keys), jnp.int32)
-        for j in range(SETS):
-            local = half * SETS + j
-            length = jnp.where(
-                local_group == local, length_ref[band * (2 * SETS) + local], length
-            )
+        for side in range(2):
+            for j in range(BANDS):
+                local = side * SETS + half * BANDS + j
+                length = jnp.where(
+                    local_group == local, length_ref[band * (2 * SETS) + local], length
+                )
         spread = lax.broadcasted_iota(jnp.int32, (groups, keys), 0) == key_group
         seen = jnp.dot(rows, spread.astype(jnp.bfloat16), preferred_element_type=jnp.float32)
         reach = (key_group == own) | ((key_group < own) & (seen > 0.5))
@@ -161,7 +163,7 @@
     query = mine[:, 2 * WIDE :]
     own = lax.all_to_all(
         jnp.broadcast_to(mine[None, :, : 2 * WIDE], (SETS, SLOTS, 2 * WIDE)),
-        ("yl", "x"),
+        ("x", "yl"),
         split_axis=0,
         concat_axis=0,
         tiled=True,

time: 68.6 us -> 68.6 us (level)
  the two profiles are of different devices: /device:TPU:10 before, /device:TPU:8 now
where the time goes in v5:
time: 68.6 us; the launch traced here: 68.2 us
  blocking collectives  42 us (61%)
  starting transfers between devices  20.7 us (30%)
  Pallas kernels  3.44 us (5%)
  local copies, waits for them, and re-layouts  1.08 us (2%)
  other arithmetic  0.86 us (1%)
    all_to_all x1, blocking collectives, local(): mine = lax.all_to_all(mine, 'head', split_axis=0, concat_axis=0, tiled=True)  19.5 us
    all_to_all x1, blocking collectives, local(): lax.all_to_all(partial.reshape(BANDS * SETS, ROWS, WIDE + HD), ('yh', 'he...  17.7 us
    ppermute x3, starting transfers between devices, local(): lax.ppermute(query, 'yh', [(i, (i + k) % BANDS) for i in range(BANDS)])  14.8 us
    all_to_all x1, starting transfers between devices, local(): lax.all_to_all(jnp.broadcast_to(mine[None, :, :2 * WIDE], (SETS, SLOTS, 2...  5.9 us
    all_gather x2, blocking collectives, local(): lax.all_gather(a.reshape(-1, 2 * WIDE), 'core', axis=0, tiled=True)  4.73 us
    pallas_call x1, Pallas kernels, local(): pl.pallas_call(attend, out_shape=jax.ShapeDtypeStruct((BANDS, SLOTS, WIDE...  1.45 us
  transfers between devices with their start and end apart: 4, of which 0 were waited for; matrix products, arithmetic and copies ran while one was open for 0% of the time, Pallas kernels for 1%

profile of v5, /device:TPU:8, one launch (start us, length us, event | category | flops | bytes accessed | tf_op | source)
XLA Modules:
  0.0 68.2 jit_solution(11037879100186907361)
XLA Ops:
  0.0 0.9 %pad_maximum_fusion = bf16[8,8,1152]{2,1,0:T(8,128)(2,1)S(1)} fusion(bf16[8,8,384]{2,1,0:T(8,128)(2,1)} %bitcast.18, bf16[8,8,384]{2,1,0:T(8,128)(2,1)} %bitcast.19, bf16[8,8,384]{2,1,0:T(8,128)(2,1)} %bitcast.20), kind=kLoop, calls=%fused_computation | loop fusion | flops 442368 | bytes 294912 | tf_op jit(solution)/shard_map/concatenate | solution.py:157
  0.9 19.5 %all_to_all.15 = bf16[8,8,1152]{2,1,0:T(8,128)(2,1)S(1)} all-to-all(bf16[8,8,1152]{2,1,0:T(8,128)(2,1)S(1)} %pad_maximum_fusion), channel_id=1, replica_groups=mesh['yh'=4,'yl'=2,'x'=4,'core'=2,'head'=8] {'head'}, dimensions={0} | all-to-all | bytes 294912 | tf_op jit(solution)/shard_map/all_to_all | solution.py:161
  20.4 1.0 %broadcast_in_dim.2 = bf16[8,64,768]{2,1,0:T(8,128)(2,1)} broadcast(bf16[64,768]{1,0:T(8,128)(2,1)S(1)} %slice.17), dimensions={1,2} | broadcast | bytes 884736 | tf_op jit(solution)/shard_map/broadcast_in_dim | solution.py:165
  21.4 0.0 copy-start
  21.4 0.0 copy-start.1
  21.4 0.0 copy-start.4
  21.4 0.0 copy-start.5
  21.4 0.0 copy-start.6
  21.4 0.0 copy-start.7
  21.4 5.9 %all-to-all-start.1 = ((bf16[8,64,768]{2,1,0:T(8,128)(2,1)}), bf16[8,64,768]{2,1,0:T(8,128)(2,1)S(1)}, u32[]{:S(2)}, u32[]{:S(2)}) async-start(bf16[8,64,768]{2,1,0:T(8,128)(2,1)} %broadcast_in_dim.2), calls=%async_computation.1 | async-start | bytes 1572864 | tf_op jit(solution)/shard_map/all_to_all | solution.py:164
  27.3 0.0 copy-done
  27.3 0.0 copy-done.1
  27.3 0.0 copy-done.2
  27.4 0.0 copy-done.3
  27.4 0.0 copy-done.4
  27.4 0.0 copy-done.5
  27.4 0.0 copy-done.6
  27.4 0.0 copy-done.7
  27.4 0.8 %shard_map.109 = (f32[8,512]{1,0:T(8,128)S(1)}, f32[8,3072]{1,0:T(8,128)S(1)}, f32[8,3072]{1,0:T(8,128)S(1)}) custom-call(s32[64]{0:T(128)S(1)} %copy-done.4, s32[64]{0:T(128)S(1)} %copy-done.5, f32[32]{0:T(128)S(1)} %copy-done.6, f32[32]{0:T(128)S(1)} %copy-done.7, s32[64,64]{1,0:T(8,128)S(1)} %copy-done.3, f32[8,3072]{1,0:T(8,128)S(1)} %copy-done.1, ...), custom_call_target="tpu_custom_call" | custom-call | tf_op jit(solution)/shard_map/pallas_call | solution.py:176
  28.2 6.8 %collective-permute-start = (bf16[64,384]{1,0:T(8,128)(2,1)S(1)}, bf16[64,384]{1,0:T(8,128)(2,1)S(1)}, u32[]{:S(2)}, u32[]{:S(2)}) collective-permute-start(bf16[64,384]{1,0:T(8,128)(2,1)S(1)} %slice.16.refs_0_), channel_id=1, source_target_pairs={{0,256},{128,384},{256,0},{384,128},{1,257},{129,385},{257,1},{385... | collective-permute-start | bytes 147464 | tf_op jit(solution)/shard_map/ppermute | solution.py:172
  35.1 2.7 %collective-permute-start.1 = (bf16[64,384]{1,0:T(8,128)(2,1)S(1)}, bf16[64,384]{1,0:T(8,128)(2,1)S(1)}, u32[]{:S(2)}, u32[]{:S(2)}) collective-permute-start(bf16[64,384]{1,0:T(8,128)(2,1)S(1)} %slice.16.refs_0_), channel_id=1, source_target_pairs={{0,128},{128,256},{256,384},{384,0},{1,129},{129,257},{257,385},{3... | collective-permute-start | bytes 147464 | tf_op jit(solution)/shard_map/ppermute | solution.py:172
  37.8 5.3 %collective-permute-start.2 = (bf16[64,384]{1,0:T(8,128)(2,1)S(1)}, bf16[64,384]{1,0:T(8,128)(2,1)S(1)}, u32[]{:S(2)}, u32[]{:S(2)}) collective-permute-start(bf16[64,384]{1,0:T(8,128)(2,1)S(1)} %slice.16.refs_0_), channel_id=1, source_target_pairs={{0,384},{128,0},{256,128},{384,256},{1,385},{129,1},{257,129},{385... | collective-permute-start | bytes 147464 | tf_op jit(solution)/shard_map/ppermute | solution.py:172
  43.1 0.0 all-to-all-done.1
  43.1 0.1 fusion
  43.1 2.4 %all_gather.6.refs_4_ = bf16[512,768]{1,0:T(8,128)(2,1)S(1)} all-gather(bf16[256,768]{1,0:T(8,128)(2,1)S(1)} %bitcast.15), channel_id=1, replica_groups=mesh['yh'=4,'yl'=2,'x'=4,'core'=2,'head'=8] {'core'}, dimensions={0}, use_global_device_ids=true | all-gather | bytes 1179648 | tf_op jit(solution)/shard_map/all_gather | solution.py:185
  45.5 2.4 %all_gather.7.refs_5_ = bf16[512,768]{1,0:T(8,128)(2,1)S(1)} all-gather(bf16[256,768]{1,0:T(8,128)(2,1)S(1)} %bitcast.14), channel_id=1, replica_groups=mesh['yh'=4,'yl'=2,'x'=4,'core'=2,'head'=8] {'core'}, dimensions={0}, use_global_device_ids=true | all-gather | bytes 1179648 | tf_op jit(solution)/shard_map/all_gather | solution.py:185
  47.9 0.0 collective-permute-done.refs_1_
  47.9 0.0 collective-permute-done.1.refs_2_
  47.9 0.0 collective-permute-done.2.refs_3_
  47.9 1.4 %shard_map.110 = bf16[4,64,512]{2,1,0:T(8,128)(2,1)S(1)} custom-call(bf16[64,384]{1,0:T(8,128)(2,1)S(1)} %slice.16.refs_0_, bf16[64,384]{1,0:T(8,128)(2,1)S(1)} %collective-permute-done.refs_1_, bf16[64,384]{1,0:T(8,128)(2,1)S(1)} %collective-permute-done.1.refs_2_, bf16[64,384]{1,0:T(8,128)(2,1)S(1)} %collective-permute-done.2.refs_3_, ...), custom_call_target="tpu_custom_call" | custom-call | tf_op jit(solution)/shard_map/pallas_call | solution.py:188
  49.3 17.7 %all_to_all.16.part_ref = bf16[32,8,512]{2,1,0:T(8,128)(2,1)S(1)} all-to-all(bf16[32,8,512]{2,1,0:T(8,128)(2,1)S(1)} %bitcast.13), channel_id=1, replica_groups=mesh['yh'=4,'yl'=2,'x'=4,'core'=2,'head'=8] {'yh','head'}, dimensions={0} | all-to-all | bytes 524288 | tf_op jit(solution)/shard_map/all_to_all | solution.py:195
  67.1 1.2 %shard_map.111 = f32[8,3072]{1,0:T(8,128)} custom-call(bf16[32,8,512]{2,1,0:T(8,128)(2,1)S(1)} %all_to_all.16.part_ref, f32[8,3072]{1,0:T(8,128)S(1)} %get-tuple-element.9.base_ref, f32[8,3072]{1,0:T(8,128)S(1)} %get-tuple-element.10.slope_ref), custom_call_target="tpu_custom_call" | custom-call | tf_op jit(solution)/shard_map/pallas_call | solution.py:202
  (4 shorter events, 0.0 us)
Async XLA Ops:
  21.4 6.0 %copy-start = (f32[32,3072]{1,0:T(8,128)S(1)}, f32[32,3072]{1,0:T(8,128)}, u32[]{:S(2)}) copy-start(f32[32,3072]{1,0:T(8,128)} %gate_ref.1) | copy-start | bytes 1179652
  21.4 6.0 %copy-start.1 = (f32[8,3072]{1,0:T(8,128)S(1)}, f32[8,3072]{1,0:T(8,128)}, u32[]{:S(2)}) copy-start(f32[8,3072]{1,0:T(8,128)} %latent_ref.1) | copy-start | bytes 294916
  21.4 6.0 %copy-start.2 = (f32[8,3072]{1,0:T(8,128)S(1)}, f32[8,3072]{1,0:T(8,128)}, u32[]{:S(2)}) copy-start(f32[8,3072]{1,0:T(8,128)} %noise_ref.1) | copy-start | bytes 294916
  21.4 6.0 %copy-start.3 = (s32[64,64]{1,0:T(8,128)S(1)}, s32[64,64]{1,0:T(8,128)}, u32[]{:S(2)}) copy-start(s32[64,64]{1,0:T(8,128)} %visible_ref.1) | copy-start | bytes 49156
  21.4 6.0 %copy-start.4 = (s32[64]{0:T(128)S(1)}, s32[64]{0:T(128)}, u32[]{:S(2)}) copy-start(s32[64]{0:T(128)} %time_ref.1) | copy-start | bytes 772
  21.4 6.0 %copy-start.5 = (s32[64]{0:T(128)S(1)}, s32[64]{0:T(128)}, u32[]{:S(2)}) copy-start(s32[64]{0:T(128)} %length_ref.1) | copy-start | bytes 772
  21.4 6.0 %copy-start.6 = (f32[32]{0:T(128)S(1)}, f32[32]{0:T(128)}, u32[]{:S(2)}) copy-start(f32[32]{0:T(128)} %step_ref.1) | copy-start | bytes 388
  21.4 6.0 %copy-start.7 = (f32[32]{0:T(128)S(1)}, f32[32]{0:T(128)}, u32[]{:S(2)}) copy-start(f32[32]{0:T(128)} %level_ref.1) | copy-start | bytes 388
  21.4 21.6 %all-to-all-start.1 = ((bf16[8,64,768]{2,1,0:T(8,128)(2,1)}), bf16[8,64,768]{2,1,0:T(8,128)(2,1)S(1)}, u32[]{:S(2)}, u32[]{:S(2)}) async-start(bf16[8,64,768]{2,1,0:T(8,128)(2,1)} %broadcast_in_dim.2), calls=%async_computation.1 | async-start | bytes 1572864 | tf_op jit(solution)/shard_map/all_to_all | solution.py:164
  28.2 19.6 %collective-permute-start = (bf16[64,384]{1,0:T(8,128)(2,1)S(1)}, bf16[64,384]{1,0:T(8,128)(2,1)S(1)}, u32[]{:S(2)}, u32[]{:S(2)}) collective-permute-start(bf16[64,384]{1,0:T(8,128)(2,1)S(1)} %slice.16.refs_0_), channel_id=1, source_target_pairs={{0,256},{128,384},{256,0},{384,128},{1,257},{129,385},{257,1},{385... | collective-permute-start | bytes 147464 | tf_op jit(solution)/shard_map/ppermute | solution.py:172
  35.1 12.8 %collective-permute-start.1 = (bf16[64,384]{1,0:T(8,128)(2,1)S(1)}, bf16[64,384]{1,0:T(8,128)(2,1)S(1)}, u32[]{:S(2)}, u32[]{:S(2)}) collective-permute-start(bf16[64,384]{1,0:T(8,128)(2,1)S(1)} %slice.16.refs_0_), channel_id=1, source_target_pairs={{0,128},{128,256},{256,384},{384,0},{1,129},{129,257},{257,385},{3... | collective-permute-start | bytes 147464 | tf_op jit(solution)/shard_map/ppermute | solution.py:172
  37.8 10.1 %collective-permute-start.2 = (bf16[64,384]{1,0:T(8,128)(2,1)S(1)}, bf16[64,384]{1,0:T(8,128)(2,1)S(1)}, u32[]{:S(2)}, u32[]{:S(2)}) collective-permute-start(bf16[64,384]{1,0:T(8,128)(2,1)S(1)} %slice.16.refs_0_), channel_id=1, source_target_pairs={{0,384},{128,0},{256,128},{384,256},{1,385},{129,1},{257,129},{385... | collective-permute-start | bytes 147464 | tf_op jit(solution)/shard_map/ppermute | solution.py:172
